TPU v7x, 512 devices: a whole 4x8x8 slice. The times are simulated.
512 devices in a mesh: row: 32 (over z, x), col: 16 (over y, core).
Axes of the slice: x: 4, y: 8, z: 8, core: 2. Of those that a mesh axis runs over, the one named last changes fastest.
Arguments:
- features: bfloat16 [65536, 128], P(('row', 'col')), may hold values from -6 to 6
- cotangent: bfloat16 [65536, 128], P(('row', 'col')), may hold values from -6 to 6
- self_weight: bfloat16 [128, 128], replicated, may hold values from -0.5 to 0.5
- neigh_weight: bfloat16 [128, 128], replicated, may hold values from -0.5 to 0.5
- degrees: int32 [65536], P(('row', 'col')), may hold values from 512 to 2048
- adjacency: int32 [32, 16, 64, 128, 128], P('row', 'col'), may hold values 0 or 1
- tile_rows: int32 [32, 16, 64], P('row', 'col'), may hold values from 0 to 31
- tile_cols: int32 [32, 16, 64], P('row', 'col'), may hold values from 0 to 15
- tile_count: int32 [32, 16], P('row', 'col'), may hold values from 32 to 64, as said below
Outputs:
- hidden: bfloat16 [65536, 128], P(('row', 'col'))
- grad_features: bfloat16 [65536, 128], P(('row', 'col'))
- grad_self: float32 [128, 128], replicated
- grad_neigh: float32 [128, 128], replicated
Inputs may be any that keep to these rules, and one draw needn't show every extreme that they name: `tile_count`: each device has between 64 // 2 (at least 1) and 64 live slots; in every draw some device has exactly 64. `tile_rows`: only a device's first tile_count slots are live; places may repeat. `tile_cols`: only a device's first tile_count slots are live; places may repeat.
All inputs are finite; a program needn't handle non-finite values. No bound on the sum of `adjacency` on one device may be relied on, other than what follows from the above.
Results may differ from a plain program's by a relative error of at most 0.024.
Values may be sent and summed in bfloat16 or wider, within the bound.
No kernel may reach another device: no remote copies, remote signals or barrier semaphores. Data moves between devices by JAX's collectives and lax.ppermute only.
A program may use at most 64 MiB of HBM per device.

v0:
```python
import jax
import jax.numpy as jnp
from jax import lax
from jax.sharding import PartitionSpec as P


def tile_sums(tile_bits, pick_blocks, place_blocks, is_live, source, out_blocks, transpose):
    edge = tile_bits.shape[-1]
    source_blocks = source.reshape(-1, edge, source.shape[-1])
    chosen = jnp.take(source_blocks, pick_blocks, axis=0)
    if transpose:
        products = jnp.einsum("kji,kjf->kif", tile_bits, chosen, preferred_element_type=jnp.float32)
    else:
        products = jnp.einsum("kij,kjf->kif", tile_bits, chosen, preferred_element_type=jnp.float32)
    targets = jnp.arange(out_blocks, dtype=jnp.int32)
    select = jnp.where(
        (place_blocks[None, :] == targets[:, None]) & is_live[None, :], 1.0, 0.0
    ).astype(jnp.float32)
    summed = jnp.einsum("bk,kif->bif", select, products, precision=lax.Precision.HIGHEST)
    return summed.reshape(out_blocks * edge, source.shape[-1])


def dense_layer(node_feats, node_cot, mixed, self_weight, neigh_weight, inverse):
    linear = jnp.dot(node_feats, self_weight, preferred_element_type=jnp.float32) + jnp.dot(
        mixed, neigh_weight, preferred_element_type=jnp.float32
    )
    sigma = jax.nn.sigmoid(linear)
    hidden = (linear * sigma).astype(jnp.bfloat16)
    grad_linear = (node_cot.astype(jnp.float32) * sigma * (1.0 + linear * (1.0 - sigma))).astype(
        jnp.bfloat16
    )
    grad_mixed = (
        jnp.dot(grad_linear, neigh_weight.T, preferred_element_type=jnp.float32) * inverse
    ).astype(jnp.bfloat16)
    return (hidden, grad_linear, grad_mixed)


def body(
    features,
    cotangent,
    self_weight,
    neigh_weight,
    degrees,
    adjacency,
    tile_rows,
    tile_cols,
    tile_count,
):
    edge = adjacency.shape[-1]
    capacity = adjacency.shape[2]
    tile_bits = adjacency.reshape(capacity, edge, edge).astype(jnp.bfloat16)
    row_ids = tile_rows.reshape(capacity)
    col_ids = tile_cols.reshape(capacity)
    is_live = jnp.arange(capacity, dtype=jnp.int32) < tile_count.reshape(())
    owned = features.shape[0]
    row_blocks = lax.axis_size("row") * owned // edge
    col_blocks = lax.axis_size("col") * owned // edge
    inverse = lax.rsqrt(jnp.maximum(degrees, 1).astype(jnp.float32))[:, None]
    source = lax.all_gather(features, "col", axis=0, tiled=True)
    partial_value = tile_sums(
        tile_bits, col_ids, row_ids, is_live, source, row_blocks, False
    ).astype(jnp.bfloat16)
    summed = lax.psum_scatter(partial_value, "row", scatter_dimension=0, tiled=True).astype(
        jnp.float32
    )
    mixed = (summed * inverse).astype(jnp.bfloat16)
    hidden, grad_linear, grad_mixed = dense_layer(
        features, cotangent, mixed, self_weight, neigh_weight, inverse
    )
    spread = lax.all_gather(grad_mixed, "row", axis=0, tiled=True)
    back_partial = tile_sums(tile_bits, row_ids, col_ids, is_live, spread, col_blocks, True).astype(
        jnp.bfloat16
    )
    returned = lax.psum_scatter(back_partial, "col", scatter_dimension=0, tiled=True).astype(
        jnp.float32
    )
    grad_features = (
        jnp.dot(grad_linear, self_weight.T, preferred_element_type=jnp.float32) + returned
    ).astype(jnp.bfloat16)
    local_self = jnp.einsum("nf,ng->fg", features, grad_linear, preferred_element_type=jnp.float32)
    local_neigh = jnp.einsum("nf,ng->fg", mixed, grad_linear, preferred_element_type=jnp.float32)
    grad_self, grad_neigh = lax.psum((local_self, local_neigh), ("row", "col"))
    return (hidden, grad_features, grad_self, grad_neigh)


def solution(mesh):
    in_specs = (
        P(("row", "col"), None),
        P(("row", "col"), None),
        P(),
        P(),
        P(("row", "col")),
        P("row", "col", None, None, None),
        P("row", "col", None),
        P("row", "col", None),
        P("row", "col"),
    )
    out_specs = (P(("row", "col"), None), P(("row", "col"), None), P(), P())
    return jax.shard_map(body, mesh=mesh, in_specs=in_specs, out_specs=out_specs, check_vma=False)
```

profile of v0, /device:TPU:1, one launch (start us, length us, event | category | flops | bytes accessed | tf_op | source)
XLA Modules:
  0.0 682.0 jit_solution(14779230361226520241)
XLA Ops:
  7.2 0.0 copy-start
  7.2 0.0 reduce-scatter.3.cloned.1.call-start
  7.2 0.7 fusion.41
  7.9 0.7 compare_and_fusion.1
  8.5 22.7 %all_gather.6 = bf16[2048,128]{1,0:T(8,128)(2,1)S(1)} all-gather(bf16[128,128]{1,0:T(8,128)(2,1)} %param.9), channel_id=1, replica_groups=mesh['row'=32,'col'=16] {'col'}, dimensions={0}, use_global_device_ids=true | all-gather | bytes 557056 | tf_op jit(solution)/shard_map/all_gather | solution.py:59
  31.2 0.9 gather_fusion
  32.2 5.9 fusion.6
  38.1 0.0 copy-start.3
  38.1 5.4 copy.18
  44.2 0.0 copy-done.3
  44.2 4.3 fusion.12
  48.5 0.0 copy-start.6
  48.5 0.0 copy-start.1
  48.5 0.0 copy-start.2
  48.5 0.0 copy-start.5
  48.5 1.4 copy.15
  49.9 0.0 reduce-scatter.3.cloned.1.call-update
  49.9 0.0 all-gather.2.cloned.1.call-start
  50.0 0.0 copy-done.6
  50.0 0.0 copy-done.1
  50.0 0.0 copy-done.2
  50.0 0.1 fusion.49
  50.2 214.5 %reduce-scatter.3.cloned.1.call-done = bf16[128,128]{1,0:T(8,128)(2,1)} async-done(((bf16[4096,128]{1,0:T(8,128)(2,1)}), bf16[128,128]{1,0:T(8,128)(2,1)}) %reduce-scatter.3.cloned.1.call-update) | async-done | bytes 32784 | tf_op jit(solution)/shard_map/reduce_scatter | solution.py:63
  264.6 0.0 copy-done
  264.6 0.0 copy-done.5
  264.6 1.6 multiply_convert_fusion
  266.2 0.8 fusion.19
  267.0 0.0 all-gather.2.cloned.1.call-update
  267.0 0.0 all-reduce.3.cloned.1.call-start
  267.1 0.8 convolution_bitcast_fusion
  267.9 1.6 fusion.28
  269.6 0.0 all-reduce.3.cloned.1.call-update
  269.6 0.0 reduce-scatter.5.cloned.1.call-start
  269.7 79.5 %all-gather.2.cloned.1.call-done = bf16[4096,128]{1,0:T(8,128)(2,1)} async-done(((bf16[128,128]{1,0:T(8,128)(2,1)}), bf16[4096,128]{1,0:T(8,128)(2,1)}) %all-gather.2.cloned.1.call-update) | async-done | bytes 1048592 | tf_op jit(solution)/shard_map/all_gather | solution.py:70
  349.2 2.2 gather_fusion.1
  351.4 5.1 fusion.4
  356.5 0.0 copy-start.4
  356.5 5.4 copy.19
  361.9 0.0 copy-done.4
  361.9 4.3 fusion.15
  366.1 0.9 copy.16
  367.1 0.0 reduce-scatter.5.cloned.1.call-update
  367.1 252.2 %all-reduce.3.cloned.1.call-done = (f32[128,128]{0,1:T(8,128)}, f32[128,128]{1,0:T(8,128)}) async-done(((f32[128,128]{0,1:T(8,128)}, f32[128,128]{1,0:T(8,128)}), (f32[128,128]{0,1:T(8,128)}, f32[128,128]{1,0:T(8,128)})) %all-reduce.3.cloned.1.call-update) | async-done | bytes 131088 | tf_op jit(solution)/shard_map/psum | solution.py:82
  619.3 1.6 copy.17
  620.9 51.6 %reduce-scatter.5.cloned.1.call-done = bf16[128,128]{1,0:T(8,128)(2,1)} async-done(((bf16[2048,128]{1,0:T(8,128)(2,1)}), bf16[128,128]{1,0:T(8,128)(2,1)}) %reduce-scatter.5.cloned.1.call-update) | async-done | bytes 32784 | tf_op jit(solution)/shard_map/reduce_scatter | solution.py:74
  672.5 1.5 fusion.18
  674.0 1.5 copy.23
  (6 shorter events, 0.0 us)
Async XLA Ops:
  7.2 257.5 %copy-start = (bf16[128,128]{1,0:T(8,128)(2,1)S(1)}, bf16[128,128]{1,0:T(8,128)(2,1)}, u32[]{:S(2)}) copy-start(bf16[128,128]{1,0:T(8,128)(2,1)} %param.12) | copy-start | bytes 98308
  7.2 257.4 %reduce-scatter.3.cloned.1.call-start = ((), (), s32[]{:S(2)}) async-start(), calls=%async_computation.2 | async-start | bytes 1081344 | tf_op jit(solution)/shard_map/reduce_scatter | solution.py:63
  38.1 6.1 copy-start.3
  48.5 1.5 copy-start.6
  48.5 1.5 copy-start.1
  48.5 1.5 copy-start.2
  48.5 216.1 %copy-start.5 = (bf16[128,128]{1,0:T(8,128)(2,1)S(1)}, bf16[128,128]{1,0:T(8,128)(2,1)}, u32[]{:S(2)}) copy-start(bf16[128,128]{1,0:T(8,128)(2,1)} %param.10) | copy-start | bytes 98308
  49.9 299.3 %all-gather.2.cloned.1.call-start = ((), (), s32[]{:S(2)}) async-start(), calls=%async_computation.3 | async-start | bytes 1081344 | tf_op jit(solution)/shard_map/all_gather | solution.py:70
  267.0 352.3 %all-reduce.3.cloned.1.call-start = ((), (), s32[]{:S(2)}) async-start(), calls=%async_computation.5 | async-start | bytes 262144 | tf_op jit(solution)/shard_map/psum | solution.py:82
  269.6 402.9 %reduce-scatter.5.cloned.1.call-start = ((), (), s32[]{:S(2)}) async-start(), calls=%async_computation.4 | async-start | bytes 557056 | tf_op jit(solution)/shard_map/reduce_scatter | solution.py:74
  356.5 5.4 copy-start.4
Sparse Core Ops, SparseCore 0:
  50.1 214.5 reduce-scatter.2
  268.4 80.7 all-gather.1
  355.0 264.2 all-reduce.2
  622.2 50.2 reduce-scatter.4
where the time goes:
time: 684 us; the launch traced here: 682 us
  waiting for transfers between devices  598 us (87%)
  matrix products  26.1 us (4%)
  blocking collectives  22.7 us (3%)
  local copies, waits for them, and re-layouts  19.3 us (3%)
  between operations  14.6 us (2%)
    psum x1, waiting for transfers between devices, body(): grad_self, grad_neigh = lax.psum((local_self, local_neigh), ('row', 'col'))  252 us
    reduce_scatter x1, waiting for transfers between devices, body(): lax.psum_scatter(partial_value, 'row', scatter_dimension=0, tiled=True)  214 us
    all_gather x1, waiting for transfers between devices, body(): spread = lax.all_gather(grad_mixed, 'row', axis=0, tiled=True)  79.5 us
    reduce_scatter x1, waiting for transfers between devices, body(): lax.psum_scatter(back_partial, 'col', scatter_dimension=0, tiled=True)  51.6 us
    all_gather x1, blocking collectives, body(): source = lax.all_gather(features, 'col', axis=0, tiled=True)  22.7 us
  transfers between devices with their start and end apart: 4, of which 4 were waited for; matrix products, arithmetic and copies ran while one was open for 3% of the time, Pallas kernels for 0%

commit v1 on v0

v1 whole, which is shorter than its diff:
```python
import jax
import jax.numpy as jnp
from jax import lax
from jax.experimental import pallas as pl
from jax.experimental.pallas import tpu as pltpu
from jax.sharding import Mesh
from jax.sharding import PartitionSpec as P

NZ, NX, NY, NC = 8, 4, 8, 2
ALL = ("z", "x", "y", "core")
ROW = ("z", "x")
COL = ("y", "core")
B = 128
F = 128
GROUP = 8
WG = 16
BF = jnp.bfloat16
F32 = jnp.float32
VMEM = pl.BlockSpec(memory_space=pltpu.VMEM)
SMEM = pl.BlockSpec(memory_space=pltpu.SMEM)
PARAMS = pltpu.CompilerParams(vmem_limit_bytes=24 * 1024 * 1024)


def dot(a, b, contract=((1,), (0,))):
    return lax.dot_general(a, b, (contract, ((), ())), preferred_element_type=F32)


def split(value):
    high = value.astype(BF)
    low = (value - high.astype(F32)).astype(BF)
    return high, low


def joined(pair, rows):
    return pair[:rows].astype(F32) + pair[rows:].astype(F32)


def forward_kernel(rows, cols, count, tiles, source, partial, bits, acc):
    step = pl.program_id(0)
    last = pl.num_programs(0) - 1

    @pl.when(step == 0)
    def _():
        acc[...] = jnp.zeros_like(acc)

    products = []
    for i in range(GROUP):
        k = step * GROUP + i
        tile = tiles[i].astype(F32).astype(BF)
        bits[i] = tile
        products.append(dot(tile, source[cols[k]]))
    for i in range(GROUP):
        k = step * GROUP + i
        b = rows[k]
        place = jnp.where(k < count[0], (b % NX) * NZ + b // NX, NX * NZ)
        acc[place] += products[i]

    @pl.when(step == last)
    def _():
        partial[...] = acc[: NX * NZ].astype(BF)


def forward_sums(rows, cols, count, tiles, source):
    slots = tiles.shape[0]
    return pl.pallas_call(
        forward_kernel,
        grid=(slots // GROUP,),
        in_specs=[
            SMEM,
            SMEM,
            SMEM,
            pl.BlockSpec((GROUP, B, B), lambda i: (i, 0, 0)),
            pl.BlockSpec((NY * NC, B, F), lambda i: (0, 0, 0)),
        ],
        out_specs=[
            pl.BlockSpec((NX * NZ, B, F), lambda i: (0, 0, 0)),
            pl.BlockSpec((GROUP, B, B), lambda i: (i, 0, 0)),
        ],
        out_shape=[
            jax.ShapeDtypeStruct((NX * NZ, B, F), BF),
            jax.ShapeDtypeStruct((slots, B, B), BF),
        ],
        scratch_shapes=[pltpu.VMEM((NX * NZ + 1, B, F), F32)],
        compiler_params=PARAMS,
        name="forward_sums",
    )(rows, cols, count, tiles, source)


def dense_kernel(
    pieces, features, cotangent, self_weight, neigh_weight, inv_col, inv_row, hidden, base, payload
):
    total = pieces[0].astype(F32)
    for i in range(1, NZ):
        total += pieces[i].astype(F32)
    feats = features[...]
    mixed = (total * inv_col[...]).astype(BF)
    linear = dot(feats, self_weight[...]) + dot(mixed, neigh_weight[...])
    sigma = jax.nn.sigmoid(linear)
    hidden[...] = (linear * sigma).astype(BF)
    grad = (cotangent[...].astype(F32) * sigma * (1.0 + linear * (1.0 - sigma))).astype(BF)
    spread = (dot(neigh_weight[...], grad, ((1,), (1,))) * inv_row[...]).astype(BF)
    base[...] = dot(self_weight[...], grad, ((1,), (1,)))
    part = F // (NZ // 2)
    for i, left in enumerate((feats, mixed)):
        high, low = split(dot(left, grad, ((0,), (0,))))
        for j in range(NZ // 2):
            at = i * (NZ // 2) + j
            payload[at, pl.ds(0, B)] = spread
            payload[at, pl.ds(B, part)] = high[j * part : (j + 1) * part]
            payload[at, pl.ds(B + part, part)] = low[j * part : (j + 1) * part]


def dense_layer(pieces, features, cotangent, self_weight, neigh_weight, inv_col, inv_row):
    return pl.pallas_call(
        dense_kernel,
        in_specs=[VMEM] * 7,
        out_specs=[VMEM] * 3,
        out_shape=[
            jax.ShapeDtypeStruct((B, F), BF),
            jax.ShapeDtypeStruct((F, B), F32),
            jax.ShapeDtypeStruct((NZ, B + 64, F), BF),
        ],
        compiler_params=PARAMS,
        name="dense_layer",
    )(pieces, features, cotangent, self_weight, neigh_weight, inv_col, inv_row)


def relay_kernel(arrived, payload):
    for i in range(NZ):
        block = arrived[i, pl.ds(0, B)]
        for j in range(NX):
            payload[j, pl.ds(i * B, B)] = block
    total = joined(arrived[0, pl.ds(B, 64)], 32)
    for i in range(1, NZ):
        total += joined(arrived[i, pl.ds(B, 64)], 32)
    high, low = split(total)
    for j in range(NX):
        payload[j, pl.ds(NZ * B, WG)] = jnp.concatenate(
            [high[j * 8 : j * 8 + 8], low[j * 8 : j * 8 + 8]], 0
        )


def relay(arrived):
    return pl.pallas_call(
        relay_kernel,
        in_specs=[VMEM],
        out_specs=VMEM,
        out_shape=jax.ShapeDtypeStruct((NX, NZ * B + WG, F), BF),
        compiler_params=PARAMS,
        name="relay",
    )(arrived)


def backward_kernel(rows, cols, count, core, bits, spread, own, other, acc):
    acc[...] = jnp.zeros_like(acc)
    slots = bits.shape[0]

    def step(g, carry):
        products = []
        for i in range(GROUP):
            k = g * GROUP + i
            b = rows[k]
            source = spread[b % NX, pl.ds(pl.multiple_of((b // NX) * B, B), B)]
            products.append(dot(source, bits[k]))
        for i in range(GROUP):
            k = g * GROUP + i
            b = cols[k]
            place = jnp.where(k < count[0], (b % NC) * NY + b // NC, NY * NC)
            acc[place] += products[i]
        return carry

    lax.fori_loop(0, slots // GROUP, step, 0)
    me = core[0]
    for i in range(NY):
        own[pl.ds(i * B, B)] = acc[me * NY + i].astype(BF)
        other[pl.ds(i * B, B)] = acc[(1 - me) * NY + i].astype(BF)
    total = joined(spread[0, pl.ds(NZ * B, WG)], 8)
    for i in range(1, NX):
        total += joined(spread[i, pl.ds(NZ * B, WG)], 8)
    high, low = split(total)
    pair = jnp.concatenate([high, low], 0)
    own[pl.ds(NY * B, WG)] = pair
    other[pl.ds(NY * B, WG)] = pair


def backward_sums(rows, cols, count, core, bits, spread):
    return pl.pallas_call(
        backward_kernel,
        in_specs=[SMEM, SMEM, SMEM, SMEM, VMEM, VMEM],
        out_specs=[VMEM, VMEM],
        out_shape=[jax.ShapeDtypeStruct((NY * B + WG, B), BF)] * 2,
        scratch_shapes=[pltpu.VMEM((NY * NC + 1, F, B), F32)],
        compiler_params=PARAMS,
        name="backward_sums",
    )(rows, cols, count, core, bits, spread)


def merge_kernel(own, other, payload):
    pair = joined(own[pl.ds(NY * B, WG)], 8) + joined(other[pl.ds(NY * B, WG)], 8)
    high, low = split(pair)
    tail = jnp.concatenate([high, low], 0)
    for i in range(NY):
        at = pl.ds(i * B, B)
        payload[i, pl.ds(0, B)] = (own[at].astype(F32) + other[at].astype(F32)).astype(BF)
        payload[i, pl.ds(B, WG)] = tail


def merge(own, other):
    return pl.pallas_call(
        merge_kernel,
        in_specs=[VMEM, VMEM],
        out_specs=VMEM,
        out_shape=jax.ShapeDtypeStruct((NY, B + WG, B), BF),
        compiler_params=PARAMS,
        name="merge",
    )(own, other)


def final_kernel(arrived, base, grad_features, chunk):
    total = base[...]
    tail = joined(arrived[0, pl.ds(B, WG)], 8)
    for i in range(NY):
        total += arrived[i, pl.ds(0, B)].astype(F32)
        if i > 0:
            tail += joined(arrived[i, pl.ds(B, WG)], 8)
    grad_features[...] = total.T.astype(BF)
    for i in range(NZ * NX):
        chunk[i] = tail


def final(arrived, base):
    return pl.pallas_call(
        final_kernel,
        in_specs=[VMEM, VMEM],
        out_specs=[VMEM, VMEM],
        out_shape=[
            jax.ShapeDtypeStruct((B, F), BF),
            jax.ShapeDtypeStruct((NZ * NX, 8, F), F32),
        ],
        compiler_params=PARAMS,
        name="final",
    )(arrived, base)


def exchange(value, axis):
    return lax.all_to_all(value, axis, 0, 0, tiled=True)


def body(
    features,
    cotangent,
    self_weight,
    neigh_weight,
    degrees,
    adjacency,
    tile_rows,
    tile_cols,
    tile_count,
):
    slots = adjacency.shape[2]
    tiles = adjacency.reshape(slots, B, B)
    rows = tile_rows.reshape(slots)
    cols = tile_cols.reshape(slots)
    count = tile_count.reshape(1)
    core = lax.axis_index("core").reshape(1)
    inverse = lax.rsqrt(jnp.maximum(degrees, 1).astype(F32))

    source = lax.all_gather(features, COL, axis=0, tiled=False)
    partial, bits = forward_sums(rows, cols, count, tiles, source)
    arrived = exchange(partial.reshape(NX, NZ * B, F), "x")
    summed = jnp.sum(arrived, axis=0, dtype=F32).astype(BF)
    pieces = exchange(summed.reshape(NZ, B, F), "z")
    hidden, base, payload = dense_layer(
        pieces, features, cotangent, self_weight, neigh_weight, inverse[:, None], inverse[None, :]
    )
    spread = exchange(relay(exchange(payload, "z")), "x")
    own, other = backward_sums(rows, cols, count, core, bits, spread)
    other = lax.ppermute(other, "core", [(0, 1), (1, 0)])
    returned = exchange(merge(own, other), "y")
    grad_features, chunk = final(returned, base)
    grads = exchange(chunk, ROW).reshape(2, F, F)
    return (hidden, grad_features, grads[0], grads[1])


def solution(mesh):
    grid = Mesh(mesh.devices.reshape(NZ, NX, NY, NC), ALL)
    in_specs = (
        P(ALL, None),
        P(ALL, None),
        P(),
        P(),
        P(ALL),
        P(ROW, COL, None, None, None),
        P(ROW, COL, None),
        P(ROW, COL, None),
        P(ROW, COL),
    )
    out_specs = (P(ALL, None), P(ALL, None), P(), P())
    return jax.shard_map(body, mesh=grid, in_specs=in_specs, out_specs=out_specs, check_vma=False)
```

time: 684 us -> 141 us (0.21)
  waiting for transfers between devices: 598 us -> 21.7 us
  blocking collectives: 22.7 us -> 83.5 us
  matrix products: 26.1 us -> 0 us
  starting transfers between devices: 0.16 us -> 20.1 us
  local copies, waits for them, and re-layouts: 19.3 us -> 4.31 us
  between operations: 14.6 us -> 1.39 us
  Pallas kernels: 0 us -> 8.14 us
    reduce_scatter x2 -> x0, waiting for transfers between devices: 266 us -> none  [the longest x1 214 us: body(): lax.psum_scatter(partial_value, 'row', scatter_dimension=0, tiled=True)]
    psum x1 -> x0, waiting for transfers between devices: 252 us -> none  [body(): grad_self, grad_neigh = lax.psum((local_self, local_neigh), ('row', 'col'))]
    all_gather x1 -> x0, waiting for transfers between devices: 79.5 us -> none  [body(): spread = lax.all_gather(grad_mixed, 'row', axis=0, tiled=True)]
    all_to_all x0 -> x4, blocking collectives: none -> 60.8 us  [exchange(): return lax.all_to_all(value, axis, 0, 0, tiled=True)]
    dot_general x10 -> x0, matrix products: 26.1 us -> none  [the longest x2 8.56 us: tile_sums(): jnp.einsum('bk,kif->bif', select, products, precision=lax.Precision.HIGHEST)]
    all_to_all x0 -> x2, waiting for transfers between devices: none -> 20.5 us  [exchange(): return lax.all_to_all(value, axis, 0, 0, tiled=True)]
    all_to_all x0 -> x2, starting transfers between devices: none -> 12.8 us  [exchange(): return lax.all_to_all(value, axis, 0, 0, tiled=True)]
    dot_general x2 -> x0, local copies, waits for them, and re-layouts: 10.8 us -> none  [the longest x1 5.4 us: tile_sums(): jnp.einsum('kij,kjf->kif', tile_bits, chosen, preferred_element_type=jnp....]
  transfers between devices with their start and end apart: 4 -> 3, of which waited for: 4 -> 3; matrix products, arithmetic and copies ran while one was open for 3% -> 0% of each run, Pallas kernels for 0% -> 0%
where the time goes in v1:
time: 141 us; the launch traced here: 140 us
  blocking collectives  83.5 us (59%)
  waiting for transfers between devices  21.7 us (15%)
  starting transfers between devices  20.1 us (14%)
  Pallas kernels  8.14 us (6%)
  local copies, waits for them, and re-layouts  4.31 us (3%)
    all_to_all x4, blocking collectives, exchange(): return lax.all_to_all(value, axis, 0, 0, tiled=True)  60.8 us
    all_gather x1, blocking collectives, body(): source = lax.all_gather(features, COL, axis=0, tiled=False)  22.7 us
    all_to_all x2, waiting for transfers between devices, exchange(): return lax.all_to_all(value, axis, 0, 0, tiled=True)  20.5 us
    all_to_all x2, starting transfers between devices, exchange(): return lax.all_to_all(value, axis, 0, 0, tiled=True)  12.8 us
    ppermute x1, starting transfers between devices, body(): other = lax.ppermute(other, 'core', [(0, 1), (1, 0)])  7.28 us
    unnamed x20, local copies, waits for them, and re-layouts  3.54 us
  transfers between devices with their start and end apart: 3, of which 3 were waited for; matrix products, arithmetic and copies ran while one was open for 0% of the time, Pallas kernels for 0%

profile of v1, /device:TPU:1, one launch (start us, length us, event | category | flops | bytes accessed | tf_op | source)
XLA Modules:
  0.0 140.0 jit_solution(13035290416562728684)
XLA Ops:
  1.3 22.7 %all-gather = bf16[2048,128]{1,0:T(8,128)(2,1)S(1)} all-gather(bf16[128,128]{1,0:T(8,128)(2,1)} %features.1), channel_id=2, replica_groups=mesh['z'=8,'x'=4,'y'=8,'core'=2] {'y','core'}, dimensions={0}, use_global_device_ids=true | all-gather | bytes 557056 | tf_op jit(solution)/shard_map/all_gather | solution.py:268
  24.0 0.0 copy-start
  24.0 2.2 %copy-done = s32[1,1,64,128,128]{4,3,2,1,0:T(8,128)S(1)} copy-done((s32[1,1,64,128,128]{4,3,2,1,0:T(8,128)S(1)}, s32[1,1,64,128,128]{4,3,2,1,0:T(8,128)}, u32[]{:S(2)}) %copy-start) | copy-done | bytes 4194328
  26.2 0.0 copy-start.5
  26.2 0.7 copy-done.5
  26.8 0.0 copy-start.7
  26.8 0.7 copy-done.7
  27.5 2.8 %forward_sums.1 = (bf16[32,128,128]{2,1,0:T(8,128)(2,1)S(1)}, bf16[64,128,128]{2,1,0:T(8,128)(2,1)S(1)}) custom-call(s32[64]{0:T(128)S(1)} %bitcast.21, s32[64]{0:T(128)S(1)} %bitcast.23, s32[1]{0:T(128)} %bitcast.16.count, s32[64,128,128]{2,1,0:T(8,128)S(1)} %bitcast.18, bf16[16,128,128]{2,1,0:T(8,128)(2,1)S(1)} %bitcast.19), custom_call_target="tpu_custom_call" | custom-call | tf_op jit(solution)/shard_map/forward_sums/pallas_call | solution.py:65
  30.3 0.0 copy-start.9
  30.3 0.0 copy-start.1
  30.3 0.0 copy-start.2
  30.3 0.0 copy-start.3
  30.3 0.0 copy-start.4
  30.3 17.4 %all_to_all.30 = bf16[4,1024,128]{2,1,0:T(8,128)(2,1)S(1)} all-to-all(bf16[4,1024,128]{2,1,0:T(8,128)(2,1)S(1)} %bitcast.20), channel_id=1, replica_groups=mesh['z'=8,'x'=4,'y'=8,'core'=2] {'x'}, dimensions={0} | all-to-all | bytes 2097152 | tf_op jit(solution)/shard_map/all_to_all | solution.py:246
  47.7 0.9 reduce_sum.12
  48.6 9.3 %all-to-all-start.1 = ((bf16[8,128,128]{2,1,0:T(8,128)(2,1)}), bf16[8,128,128]{2,1,0:T(8,128)(2,1)S(1)}, u32[]{:S(2)}, u32[]{:S(2)}) async-start(bf16[8,128,128]{2,1,0:T(8,128)(2,1)} %bitcast.25), calls=%async_computation.1 | async-start | bytes 524288 | tf_op jit(solution)/shard_map/all_to_all | solution.py:246
  57.9 0.0 copy-done.9
  57.9 0.1 copy.13.inv_col
  58.1 9.7 %all-to-all-done.1.pieces = bf16[8,128,128]{2,1,0:T(8,128)(2,1)S(1)} async-done(((bf16[8,128,128]{2,1,0:T(8,128)(2,1)}), bf16[8,128,128]{2,1,0:T(8,128)(2,1)S(1)}, u32[]{:S(2)}, u32[]{:S(2)}) %all-to-all-start.1) | async-done | bytes 262176 | tf_op jit(solution)/shard_map/all_to_all | solution.py:246
  67.8 0.0 copy-done.1
  67.8 0.0 copy-done.2
  67.8 0.0 copy-done.3
  67.8 0.0 copy-done.4
  67.8 0.9 dense_layer.1
  68.7 0.0 copy-start.6
  68.7 0.0 copy-start.8
  68.7 14.4 %all_to_all.31.arrived = bf16[8,192,128]{2,1,0:T(8,128)(2,1)S(1)} all-to-all(bf16[8,192,128]{2,1,0:T(8,128)(2,1)S(1)} %get-tuple-element.16), channel_id=1, replica_groups=mesh['z'=8,'x'=4,'y'=8,'core'=2] {'z'}, dimensions={0} | all-to-all | bytes 786432 | tf_op jit(solution)/shard_map/all_to_all | solution.py:246
  83.1 1.1 relay.1
  84.2 3.5 %all-to-all-start.3 = ((bf16[4,1040,128]{2,1,0:T(8,128)(2,1)}), bf16[4,1040,128]{2,1,0:T(8,128)(2,1)S(1)}, u32[]{:S(2)}, u32[]{:S(2)}) async-start(bf16[4,1040,128]{2,1,0:T(8,128)(2,1)} %relay.1), calls=%async_computation.3 | async-start | bytes 2129920 | tf_op jit(solution)/shard_map/all_to_all | solution.py:246
  87.8 10.8 %all-to-all-done.3.spread = bf16[4,1040,128]{2,1,0:T(8,128)(2,1)S(1)} async-done(((bf16[4,1040,128]{2,1,0:T(8,128)(2,1)}), bf16[4,1040,128]{2,1,0:T(8,128)(2,1)S(1)}, u32[]{:S(2)}, u32[]{:S(2)}) %all-to-all-start.3) | async-done | bytes 1064992 | tf_op jit(solution)/shard_map/all_to_all | solution.py:246
  98.6 0.0 copy-done.6
  98.6 0.0 copy-done.8
  98.6 2.5 %backward_sums.1 = (bf16[1040,128]{1,0:T(8,128)(2,1)S(1)}, bf16[1040,128]{1,0:T(8,128)(2,1)S(1)}) custom-call(s32[64]{0:T(128)S(1)} %bitcast.22, s32[64]{0:T(128)S(1)} %bitcast.24, s32[1]{0:T(128)} %bitcast.17.count, s32[1]{0:T(128)} %bitcast.9.core, bf16[64,128,128]{2,1,0:T(8,128)(2,1)S(1)} %get-tuple-element.15.bits, ...), custom_call_target="tpu_custom_call" | custom-call | tf_op jit(solution)/shard_map/backward_sums/pallas_call | solution.py:187
  101.1 7.3 %collective-permute-start = (bf16[1040,128]{1,0:T(8,128)(2,1)S(1)}, bf16[1040,128]{1,0:T(8,128)(2,1)S(1)}, u32[]{:S(2)}, u32[]{:S(2)}) collective-permute-start(bf16[1040,128]{1,0:T(8,128)(2,1)S(1)} %get-tuple-element.18), channel_id=1, source_target_pairs={{0,1},{1,0},{2,3},{3,2},{4,5},{5,4},{6,7},{7,6},{8,9},{9,8},{10,11... | collective-permute-start | bytes 798728 | tf_op jit(solution)/shard_map/ppermute | solution.py:278
  108.4 1.1 collective-permute-done.other
  109.5 0.1 merge.1
  109.6 16.0 %all_to_all.32.arrived = bf16[8,144,128]{2,1,0:T(8,128)(2,1)S(1)} all-to-all(bf16[8,144,128]{2,1,0:T(8,128)(2,1)S(1)} %merge.1), channel_id=1, replica_groups=mesh['z'=8,'x'=4,'y'=8,'core'=2] {'y'}, dimensions={0} | all-to-all | bytes 589824 | tf_op jit(solution)/shard_map/all_to_all | solution.py:246
  125.6 0.7 final.1
  126.4 13.0 %all_to_all.33 = f32[32,8,128]{2,1,0:T(8,128)S(1)} all-to-all(f32[32,8,128]{2,1,0:T(8,128)S(1)} %get-tuple-element.21), channel_id=1, replica_groups=mesh['z'=8,'x'=4,'y'=8,'core'=2] {'z','x'}, dimensions={0} | all-to-all | bytes 262144 | tf_op jit(solution)/shard_map/all_to_all | solution.py:246
  139.4 0.7 slice_bitcast_fusion
  (1 shorter events, 0.0 us)
Async XLA Ops:
  24.0 2.2 %copy-start = (s32[1,1,64,128,128]{4,3,2,1,0:T(8,128)S(1)}, s32[1,1,64,128,128]{4,3,2,1,0:T(8,128)}, u32[]{:S(2)}) copy-start(s32[1,1,64,128,128]{4,3,2,1,0:T(8,128)} %param.14) | copy-start | bytes 12582916
  26.2 0.7 copy-start.5
  26.8 0.7 copy-start.7
  30.3 27.6 %copy-start.9 = (s32[128]{0:T(128)S(1)}, s32[128]{0:T(128)}, u32[]{:S(2)}) copy-start(s32[128]{0:T(128)} %param.13) | copy-start | bytes 1540
  30.3 37.5 %copy-start.1 = (bf16[128,128]{1,0:T(8,128)(2,1)S(1)}, bf16[128,128]{1,0:T(8,128)(2,1)}, u32[]{:S(2)}) copy-start(bf16[128,128]{1,0:T(8,128)(2,1)} %features.1) | copy-start | bytes 98308
  30.3 37.5 %copy-start.2 = (bf16[128,128]{1,0:T(8,128)(2,1)S(1)}, bf16[128,128]{1,0:T(8,128)(2,1)}, u32[]{:S(2)}) copy-start(bf16[128,128]{1,0:T(8,128)(2,1)} %cotangent.1) | copy-start | bytes 98308
  30.3 37.4 %copy-start.3 = (bf16[128,128]{1,0:T(8,128)(2,1)S(1)}, bf16[128,128]{1,0:T(8,128)(2,1)}, u32[]{:S(2)}) copy-start(bf16[128,128]{1,0:T(8,128)(2,1)} %self_weight.1) | copy-start | bytes 98308
  30.3 37.4 %copy-start.4 = (bf16[128,128]{1,0:T(8,128)(2,1)S(1)}, bf16[128,128]{1,0:T(8,128)(2,1)}, u32[]{:S(2)}) copy-start(bf16[128,128]{1,0:T(8,128)(2,1)} %neigh_weight.1) | copy-start | bytes 98308
  48.6 19.1 %all-to-all-start.1 = ((bf16[8,128,128]{2,1,0:T(8,128)(2,1)}), bf16[8,128,128]{2,1,0:T(8,128)(2,1)S(1)}, u32[]{:S(2)}, u32[]{:S(2)}) async-start(bf16[8,128,128]{2,1,0:T(8,128)(2,1)} %bitcast.25), calls=%async_computation.1 | async-start | bytes 524288 | tf_op jit(solution)/shard_map/all_to_all | solution.py:246
  68.7 29.9 %copy-start.6 = (s32[1,1,64]{2,1,0:T(1,128)S(1)}, s32[1,1,64]{2,1,0:T(1,128)}, u32[]{:S(2)}) copy-start(s32[1,1,64]{2,1,0:T(1,128)} %param.15) | copy-start | bytes 772
  68.7 29.9 %copy-start.8 = (s32[1,1,64]{2,1,0:T(1,128)S(1)}, s32[1,1,64]{2,1,0:T(1,128)}, u32[]{:S(2)}) copy-start(s32[1,1,64]{2,1,0:T(1,128)} %param.16) | copy-start | bytes 772
  84.2 14.3 %all-to-all-start.3 = ((bf16[4,1040,128]{2,1,0:T(8,128)(2,1)}), bf16[4,1040,128]{2,1,0:T(8,128)(2,1)S(1)}, u32[]{:S(2)}, u32[]{:S(2)}) async-start(bf16[4,1040,128]{2,1,0:T(8,128)(2,1)} %relay.1), calls=%async_computation.3 | async-start | bytes 2129920 | tf_op jit(solution)/shard_map/all_to_all | solution.py:246
  101.1 8.4 %collective-permute-start = (bf16[1040,128]{1,0:T(8,128)(2,1)S(1)}, bf16[1040,128]{1,0:T(8,128)(2,1)S(1)}, u32[]{:S(2)}, u32[]{:S(2)}) collective-permute-start(bf16[1040,128]{1,0:T(8,128)(2,1)S(1)} %get-tuple-element.18), channel_id=1, source_target_pairs={{0,1},{1,0},{2,3},{3,2},{4,5},{5,4},{6,7},{7,6},{8,9},{9,8},{10,11... | collective-permute-start | bytes 798728 | tf_op jit(solution)/shard_map/ppermute | solution.py:278

commit v2 on v1

v2 whole, which is shorter than its diff:
```python
import jax
import jax.numpy as jnp
from jax import lax
from jax.experimental import pallas as pl
from jax.experimental.pallas import tpu as pltpu
from jax.sharding import Mesh
from jax.sharding import PartitionSpec as P

NZ, NX, NY, NC = 8, 4, 8, 2
ALL = ("z", "x", "y", "core")
ROW = ("z", "x")
COL = ("y", "core")
B = 128
F = 128
WG = 32
BF = jnp.bfloat16
F32 = jnp.float32


def cost(us):
    return pl.CostEstimate(flops=0, bytes_accessed=int(us * 3.69e6), transcendentals=0)


VMEM = pl.BlockSpec(memory_space=pltpu.VMEM)
SMEM = pl.BlockSpec(memory_space=pltpu.SMEM)
PARAMS = pltpu.CompilerParams(vmem_limit_bytes=24 * 1024 * 1024)


def dot(a, b, contract=((1,), (0,))):
    return lax.dot_general(a, b, (contract, ((), ())), preferred_element_type=F32)


def forward_kernel(plan, bits, source, partial, acc):
    acc[...] = jnp.zeros_like(acc)

    slots = bits.shape[0]
    products = [dot(bits[k], source[plan[0, k]]) for k in range(slots)]
    for k in range(slots):
        acc[plan[3, k]] += products[k]
    partial[...] = acc[: NX * NZ].astype(BF)


def forward_sums(plan, bits, source):
    return pl.pallas_call(
        forward_kernel,
        in_specs=[SMEM, VMEM, VMEM],
        out_specs=VMEM,
        out_shape=jax.ShapeDtypeStruct((NX * NZ, B, F), BF),
        scratch_shapes=[pltpu.VMEM((NX * NZ + 1, B, F), F32)],
        compiler_params=PARAMS,
        cost_estimate=cost(2.7),
        name="forward_sums",
    )(plan, bits, source)


def add_kernel(arrived, summed):
    total = arrived[0].astype(F32)
    for i in range(1, arrived.shape[0]):
        total += arrived[i].astype(F32)
    summed[...] = total.astype(BF)


def add_pieces(arrived):
    return pl.pallas_call(
        add_kernel,
        in_specs=[VMEM],
        out_specs=VMEM,
        out_shape=jax.ShapeDtypeStruct(arrived.shape[1:], BF),
        compiler_params=PARAMS,
        cost_estimate=cost(0.8),
        name="add_pieces",
    )(arrived)


def dense_kernel(
    pieces,
    features,
    cotangent,
    self_weight,
    neigh_weight,
    degrees,
    hidden,
    base,
    payload,
):
    total = pieces[0].astype(F32)
    for i in range(1, NZ):
        total += pieces[i].astype(F32)
    feats = features[...]
    inverse = lax.rsqrt(jnp.maximum(degrees[...], 1).astype(F32))
    mixed = (total * jnp.broadcast_to(inverse, (B, B)).T).astype(BF)
    linear = dot(feats, self_weight[...]) + dot(mixed, neigh_weight[...])
    sigma = jax.nn.sigmoid(linear)
    hidden[...] = (linear * sigma).astype(BF)
    grad = (cotangent[...].astype(F32) * sigma * (1.0 + linear * (1.0 - sigma))).astype(BF)
    spread = (dot(neigh_weight[...], grad, ((1,), (1,))) * inverse).astype(BF)
    base[...] = dot(self_weight[...], grad, ((1,), (1,)))
    for i, left in enumerate((feats, mixed)):
        value = dot(left, grad, ((0,), (0,))).astype(BF)
        for j in range(NZ // 2):
            at = i * (NZ // 2) + j
            payload[at, pl.ds(0, B)] = spread
            payload[at, pl.ds(B, WG)] = value[j * WG : (j + 1) * WG]


def dense_layer(pieces, features, cotangent, self_weight, neigh_weight, degrees):
    return pl.pallas_call(
        dense_kernel,
        in_specs=[VMEM] * 6,
        out_specs=[VMEM] * 3,
        out_shape=[
            jax.ShapeDtypeStruct((B, F), BF),
            jax.ShapeDtypeStruct((F, B), F32),
            jax.ShapeDtypeStruct((NZ, F + WG, B), BF),
        ],
        compiler_params=PARAMS,
        cost_estimate=cost(1.1),
        name="dense_layer",
    )(pieces, features, cotangent, self_weight, neigh_weight, degrees)


def relay_kernel(arrived, payload):
    total = arrived[0, pl.ds(F, WG)].astype(F32)
    for i in range(1, NZ):
        total += arrived[i, pl.ds(F, WG)].astype(F32)
    chunk = total.astype(BF)
    for j in range(NX):
        for i in range(NZ):
            payload[j, pl.ds(i * F, F)] = arrived[i, pl.ds(0, F)]
        payload[j, pl.ds(NZ * F, WG)] = chunk


def relay(arrived):
    return pl.pallas_call(
        relay_kernel,
        in_specs=[VMEM],
        out_specs=VMEM,
        out_shape=jax.ShapeDtypeStruct((NX, NZ * F + WG, B), BF),
        compiler_params=PARAMS,
        cost_estimate=cost(1.0),
        name="relay",
    )(arrived)


def backward_kernel(plan, bits, spread, own, other, acc):
    acc[...] = jnp.zeros_like(acc)

    slots = bits.shape[0]
    products = []
    for k in range(slots):
        at = plan[1, k]
        block = spread[at // NZ, pl.ds(pl.multiple_of(at % NZ * F, F), F)]
        products.append(dot(block, bits[k]))
    for k in range(slots):
        acc[plan[2, k]] += products[k]
    total = spread[0, pl.ds(NZ * F, WG)].astype(F32)
    for i in range(1, NX):
        total += spread[i, pl.ds(NZ * F, WG)].astype(F32)
    chunk = total.astype(BF)
    me = plan[4, 0]
    for i in range(NY):
        own[pl.ds(i * F, F)] = acc[me * NY + i].astype(BF)
        other[pl.ds(i * F, F)] = acc[(1 - me) * NY + i].astype(BF)
    own[pl.ds(NY * F, WG)] = chunk
    other[pl.ds(NY * F, WG)] = chunk


def backward_sums(plan, bits, spread):
    return pl.pallas_call(
        backward_kernel,
        in_specs=[SMEM, VMEM, VMEM],
        out_specs=[VMEM, VMEM],
        out_shape=[jax.ShapeDtypeStruct((NY * F + WG, B), BF)] * 2,
        scratch_shapes=[pltpu.VMEM((NY * NC + 1, F, B), F32)],
        compiler_params=PARAMS,
        cost_estimate=cost(2.6),
        name="backward_sums",
    )(plan, bits, spread)


def merge_kernel(core, own, other, payload):
    them = 1 - core[0]
    tail = own[pl.ds(NY * F, WG)].astype(F32) + other[them, pl.ds(NY * F, WG)].astype(F32)
    for i in range(NY):
        at = pl.ds(i * F, F)
        payload[i, pl.ds(0, F)] = (own[at].astype(F32) + other[them, at].astype(F32)).astype(BF)
        payload[i, pl.ds(F, WG)] = tail.astype(BF)


def merge(core, own, other):
    return pl.pallas_call(
        merge_kernel,
        in_specs=[SMEM, VMEM, VMEM],
        out_specs=VMEM,
        out_shape=jax.ShapeDtypeStruct((NY, F + WG, B), BF),
        compiler_params=PARAMS,
        cost_estimate=cost(0.5),
        name="merge",
    )(core, own, other)


def final_kernel(arrived, base, grad_features, chunk):
    total = base[...]
    tail = arrived[0, pl.ds(F, WG)].astype(F32)
    for i in range(NY):
        total += arrived[i, pl.ds(0, F)].astype(F32)
        if i > 0:
            tail += arrived[i, pl.ds(F, WG)].astype(F32)
    grad_features[...] = total.T.astype(BF)
    for i in range(NZ):
        chunk[i] = tail.astype(BF)


def final(arrived, base):
    return pl.pallas_call(
        final_kernel,
        in_specs=[VMEM, VMEM],
        out_specs=[VMEM, VMEM],
        out_shape=[
            jax.ShapeDtypeStruct((B, F), BF),
            jax.ShapeDtypeStruct((NZ, WG, F), BF),
        ],
        compiler_params=PARAMS,
        cost_estimate=cost(0.8),
        name="final",
    )(arrived, base)


def exchange(value, axis):
    return lax.all_to_all(value, axis, 0, 0, tiled=True)


def body(
    features,
    cotangent,
    self_weight,
    neigh_weight,
    degrees,
    adjacency,
    tile_rows,
    tile_cols,
    tile_count,
):
    slots = adjacency.shape[2]
    rows = tile_rows.reshape(slots)
    cols = tile_cols.reshape(slots)
    core = lax.axis_index("core")
    slot = jnp.arange(slots, dtype=jnp.int32)
    live = slot < tile_count.reshape(())
    col_at = cols % NC * NY + cols // NC
    row_at = rows % NX * NZ + rows // NX
    plan = jnp.stack(
        [
            col_at,
            row_at,
            jnp.where(live, col_at, NY * NC),
            jnp.where(live, row_at, NX * NZ),
            jnp.full_like(slot, core),
        ]
    )
    bits = adjacency.reshape(slots, B, B).astype(BF)

    near = exchange(jnp.broadcast_to(features, (NY, B, F)), "y")
    source = lax.all_gather(near, "core", axis=0, tiled=True)
    partial = forward_sums(plan, bits, source)
    arrived = exchange(partial.reshape(NX, NZ, B, F), "x")
    pieces = exchange(add_pieces(arrived), "z")
    hidden, base, payload = dense_layer(
        pieces, features, cotangent, self_weight, neigh_weight, degrees.reshape(1, B)
    )
    spread = exchange(relay(exchange(payload, "z")), "x")
    own, other = backward_sums(plan, bits, spread)
    other = lax.all_gather(other, "core", axis=0, tiled=False)
    returned = exchange(merge(core.reshape(1), own, other), "y")
    grad_features, chunk = final(returned, base)
    grads = exchange(chunk, "z").reshape(2, F, F).astype(F32)
    return (hidden, grad_features, grads[0], grads[1])


def solution(mesh):
    grid = Mesh(mesh.devices.reshape(NZ, NX, NY, NC), ALL)
    in_specs = (
        P(ALL, None),
        P(ALL, None),
        P(),
        P(),
        P(ALL),
        P(ROW, COL, None, None, None),
        P(ROW, COL, None),
        P(ROW, COL, None),
        P(ROW, COL),
    )
    out_specs = (P(ALL, None), P(ALL, None), P(), P())
    return jax.shard_map(body, mesh=grid, in_specs=in_specs, out_specs=out_specs, check_vma=False)
```

time: 141 us -> 127 us (0.901)
  blocking collectives: 83.5 us -> 101 us
  waiting for transfers between devices: 21.7 us -> 5.35 us
  starting transfers between devices: 20.1 us -> 7.65 us
  Pallas kernels: 8.14 us -> 5.14 us
  other arithmetic: 0.91 us -> 3.36 us
  local copies, waits for them, and re-layouts: 4.31 us -> 2.22 us
    all_to_all x4 -> x6, blocking collectives: 60.8 us -> 88.4 us  [exchange(): return lax.all_to_all(value, axis, 0, 0, tiled=True)]
    all_to_all x2 -> x1, waiting for transfers between devices: 20.5 us -> 5.35 us  [exchange(): return lax.all_to_all(value, axis, 0, 0, tiled=True)]
    all_gather x1 -> x2, blocking collectives: 22.7 us -> 12.9 us  [the longest x1 7.43 us: body(): other = lax.all_gather(other, 'core', axis=0, tiled=False)]
    ppermute x1 -> x0, starting transfers between devices: 7.28 us -> none  [body(): other = lax.ppermute(other, 'core', [(0, 1), (1, 0)])]
    all_to_all x2 -> x1, starting transfers between devices: 12.8 us -> 7.65 us  [exchange(): return lax.all_to_all(value, axis, 0, 0, tiled=True)]
    unnamed x20 -> x10, local copies, waits for them, and re-layouts: 3.54 us -> 0.03 us
    convert_element_type x0 -> x1, other arithmetic: none -> 2.67 us  [body(): bits = adjacency.reshape(slots, B, B).astype(BF)]
    pallas_call x4 -> x5, Pallas kernels: 6.27 us -> 4.28 us  [the longest x1 1.67 us: forward_sums(): pl.pallas_call(forward_kernel, in_specs=[SMEM, VMEM, VMEM], out_specs=VME...]
  transfers between devices with their start and end apart: 3 -> 1, of which waited for: 3 -> 1; matrix products, arithmetic and copies ran while one was open for 0% -> 3% of each run, Pallas kernels for 0% -> 0%
where the time goes in v2:
time: 127 us; the launch traced here: 126 us
  blocking collectives  101 us (80%)
  starting transfers between devices  7.65 us (6%)
  waiting for transfers between devices  5.35 us (4%)
  Pallas kernels  5.14 us (4%)
  other arithmetic  3.36 us (3%)
  local copies, waits for them, and re-layouts  2.22 us (2%)
  between operations  1.4 us (1%)
    all_to_all x6, blocking collectives, exchange(): return lax.all_to_all(value, axis, 0, 0, tiled=True)  88.4 us
    all_to_all x1, starting transfers between devices, exchange(): return lax.all_to_all(value, axis, 0, 0, tiled=True)  7.65 us
    all_gather x1, blocking collectives, body(): other = lax.all_gather(other, 'core', axis=0, tiled=False)  7.43 us
    all_gather x1, blocking collectives, body(): source = lax.all_gather(near, 'core', axis=0, tiled=True)  5.43 us
    all_to_all x1, waiting for transfers between devices, exchange(): return lax.all_to_all(value, axis, 0, 0, tiled=True)  5.35 us
    convert_element_type x1, other arithmetic, body(): bits = adjacency.reshape(slots, B, B).astype(BF)  2.67 us
  transfers between devices with their start and end apart: 1, of which 1 were waited for; matrix products, arithmetic and copies ran while one was open for 3% of the time, Pallas kernels for 0%

profile of v2, /device:TPU:1, one launch (start us, length us, event | category | flops | bytes accessed | tf_op | source)
XLA Modules:
  0.0 126.4 jit_solution(11172842080405045728)
XLA Ops:
  0.6 1.5 %broadcast_in_dim.12 = bf16[8,128,128]{2,1,0:T(8,128)(2,1)} broadcast(bf16[128,128]{1,0:T(8,128)(2,1)} %features.1), dimensions={1,2} | broadcast | bytes 294912 | tf_op jit(solution)/shard_map/broadcast_in_dim | solution.py:263
  2.1 7.7 %all-to-all-start = ((bf16[8,128,128]{2,1,0:T(8,128)(2,1)}), bf16[8,128,128]{2,1,0:T(8,128)(2,1)S(1)}, u32[]{:S(2)}, u32[]{:S(2)}) async-start(bf16[8,128,128]{2,1,0:T(8,128)(2,1)} %broadcast_in_dim.12), calls=%async_computation | async-start | bytes 524288 | tf_op jit(solution)/shard_map/all_to_all | solution.py:230
  10.4 0.7 compare_select_fusion.6
  11.2 2.7 %convert_bitcast_fusion.bits = bf16[64,128,128]{2,1,0:T(8,128)(2,1)S(1)} fusion(s32[1,1,64,128,128]{4,3,2,1,0:T(8,128)} %param.14), kind=kLoop, calls=%fused_computation | loop fusion | flops 1048576 | bytes 6291456 | tf_op jit(solution)/shard_map/convert_element_type | solution.py:261
  13.8 5.3 %all-to-all-done = bf16[8,128,128]{2,1,0:T(8,128)(2,1)S(1)} async-done(((bf16[8,128,128]{2,1,0:T(8,128)(2,1)}), bf16[8,128,128]{2,1,0:T(8,128)(2,1)S(1)}, u32[]{:S(2)}, u32[]{:S(2)}) %all-to-all-start) | async-done | bytes 262176 | tf_op jit(solution)/shard_map/all_to_all | solution.py:230
  19.2 5.4 %all_gather.9.source = bf16[16,128,128]{2,1,0:T(8,128)(2,1)S(1)} all-gather(bf16[8,128,128]{2,1,0:T(8,128)(2,1)S(1)} %all-to-all-done), channel_id=1, replica_groups=mesh['z'=8,'x'=4,'y'=8,'core'=2] {'core'}, dimensions={0}, use_global_device_ids=true | all-gather | bytes 786432 | tf_op jit(solution)/shard_map/all_gather | solution.py:264
  24.6 1.7 %forward_sums.1 = bf16[32,128,128]{2,1,0:T(8,128)(2,1)S(1)} custom-call(s32[5,64]{1,0:T(8,128)S(1)} %stack.2.plan, bf16[64,128,128]{2,1,0:T(8,128)(2,1)S(1)} %convert_bitcast_fusion.bits, bf16[16,128,128]{2,1,0:T(8,128)(2,1)S(1)} %all_gather.9.source), custom_call_target="tpu_custom_call" | custom-call | bytes 9963000 | tf_op jit(solution)/shard_map/forward_sums/pallas_call | solution.py:44
  26.3 0.0 copy-start
  26.3 0.0 copy-start.1
  26.3 0.0 copy-start.2
  26.3 0.0 copy-start.3
  26.4 0.0 copy-start.4
  26.4 18.0 %all_to_all.35.arrived = bf16[4,8,128,128]{3,2,1,0:T(8,128)(2,1)S(1)} all-to-all(bf16[4,8,128,128]{3,2,1,0:T(8,128)(2,1)S(1)} %bitcast.38), channel_id=1, replica_groups=mesh['z'=8,'x'=4,'y'=8,'core'=2] {'x'}, dimensions={0} | all-to-all | bytes 2097152 | tf_op jit(solution)/shard_map/all_to_all | solution.py:230
  44.3 0.1 add_pieces.1
  44.5 19.1 %all_to_all.36.pieces = bf16[8,128,128]{2,1,0:T(8,128)(2,1)S(1)} all-to-all(bf16[8,128,128]{2,1,0:T(8,128)(2,1)S(1)} %add_pieces.1), channel_id=1, replica_groups=mesh['z'=8,'x'=4,'y'=8,'core'=2] {'z'}, dimensions={0} | all-to-all | bytes 524288 | tf_op jit(solution)/shard_map/all_to_all | solution.py:230
  63.5 0.0 copy-done
  63.5 0.0 copy-done.1
  63.5 0.0 copy-done.2
  63.5 0.0 copy-done.3
  63.5 0.0 copy-done.4
  63.6 0.9 dense_layer.1
  64.4 12.5 %all_to_all.37.arrived = bf16[8,160,128]{2,1,0:T(8,128)(2,1)S(1)} all-to-all(bf16[8,160,128]{2,1,0:T(8,128)(2,1)S(1)} %get-tuple-element.12), channel_id=1, replica_groups=mesh['z'=8,'x'=4,'y'=8,'core'=2] {'z'}, dimensions={0} | all-to-all | bytes 655360 | tf_op jit(solution)/shard_map/all_to_all | solution.py:230
  76.9 0.1 relay.1
  77.1 13.2 %all_to_all.38.spread = bf16[4,1056,128]{2,1,0:T(8,128)(2,1)S(1)} all-to-all(bf16[4,1056,128]{2,1,0:T(8,128)(2,1)S(1)} %relay.1), channel_id=1, replica_groups=mesh['z'=8,'x'=4,'y'=8,'core'=2] {'x'}, dimensions={0} | all-to-all | bytes 2162688 | tf_op jit(solution)/shard_map/all_to_all | solution.py:230
  90.3 1.5 %backward_sums.1 = (bf16[1056,128]{1,0:T(8,128)(2,1)S(1)}, bf16[1056,128]{1,0:T(8,128)(2,1)S(1)}) custom-call(s32[5,64]{1,0:T(8,128)S(1)} %stack.2.plan, bf16[64,128,128]{2,1,0:T(8,128)(2,1)S(1)} %convert_bitcast_fusion.bits, bf16[4,1056,128]{2,1,0:T(8,128)(2,1)S(1)} %all_to_all.38.spread), custom_call_target="tpu_custom_call" | custom-call | bytes 9594000 | tf_op jit(solution)/shard_map/backward_sums/pallas_call | solution.py:169
  91.8 7.4 %all-gather = bf16[2112,128]{1,0:T(8,128)(2,1)S(1)} all-gather(bf16[1056,128]{1,0:T(8,128)(2,1)S(1)} %get-tuple-element.14), channel_id=2, replica_groups=mesh['z'=8,'x'=4,'y'=8,'core'=2] {'core'}, dimensions={0}, use_global_device_ids=true | all-gather | bytes 811008 | tf_op jit(solution)/shard_map/all_gather | solution.py:273
  99.2 0.1 merge.1
  99.3 16.1 %all_to_all.39.arrived = bf16[8,160,128]{2,1,0:T(8,128)(2,1)S(1)} all-to-all(bf16[8,160,128]{2,1,0:T(8,128)(2,1)S(1)} %merge.1), channel_id=1, replica_groups=mesh['z'=8,'x'=4,'y'=8,'core'=2] {'y'}, dimensions={0} | all-to-all | bytes 655360 | tf_op jit(solution)/shard_map/all_to_all | solution.py:230
  115.4 0.7 final.1
  116.1 9.6 %all_to_all.40 = bf16[8,32,128]{2,1,0:T(8,128)(2,1)S(1)} all-to-all(bf16[8,32,128]{2,1,0:T(8,128)(2,1)S(1)} %get-tuple-element.17), channel_id=1, replica_groups=mesh['z'=8,'x'=4,'y'=8,'core'=2] {'z'}, dimensions={0} | all-to-all | bytes 131072 | tf_op jit(solution)/shard_map/all_to_all | solution.py:230
  125.7 0.7 fusion.6
  (2 shorter events, 0.0 us)
Async XLA Ops:
  2.1 17.1 %all-to-all-start = ((bf16[8,128,128]{2,1,0:T(8,128)(2,1)}), bf16[8,128,128]{2,1,0:T(8,128)(2,1)S(1)}, u32[]{:S(2)}, u32[]{:S(2)}) async-start(bf16[8,128,128]{2,1,0:T(8,128)(2,1)} %broadcast_in_dim.12), calls=%async_computation | async-start | bytes 524288 | tf_op jit(solution)/shard_map/all_to_all | solution.py:230
  26.3 37.2 %copy-start = (bf16[128,128]{1,0:T(8,128)(2,1)S(1)}, bf16[128,128]{1,0:T(8,128)(2,1)}, u32[]{:S(2)}) copy-start(bf16[128,128]{1,0:T(8,128)(2,1)} %features.1) | copy-start | bytes 98308
  26.3 37.2 %copy-start.1 = (bf16[128,128]{1,0:T(8,128)(2,1)S(1)}, bf16[128,128]{1,0:T(8,128)(2,1)}, u32[]{:S(2)}) copy-start(bf16[128,128]{1,0:T(8,128)(2,1)} %cotangent.1) | copy-start | bytes 98308
  26.3 37.2 %copy-start.2 = (bf16[128,128]{1,0:T(8,128)(2,1)S(1)}, bf16[128,128]{1,0:T(8,128)(2,1)}, u32[]{:S(2)}) copy-start(bf16[128,128]{1,0:T(8,128)(2,1)} %self_weight.1) | copy-start | bytes 98308
  26.3 37.2 %copy-start.3 = (bf16[128,128]{1,0:T(8,128)(2,1)S(1)}, bf16[128,128]{1,0:T(8,128)(2,1)}, u32[]{:S(2)}) copy-start(bf16[128,128]{1,0:T(8,128)(2,1)} %neigh_weight.1) | copy-start | bytes 98308
  26.4 37.2 %copy-start.4 = (s32[128]{0:T(128)S(1)}, s32[128]{0:T(128)}, u32[]{:S(2)}) copy-start(s32[128]{0:T(128)} %param.13) | copy-start | bytes 1540

commit v3 on v2

--- a/solution.py
+++ b/solution.py
@@ -81,7 +81,8 @@
     degrees,
     hidden,
     base,
-    payload,
+    column,
+    grads,
 ):
     total = pieces[0].astype(F32)
     for i in range(1, NZ):
@@ -95,28 +96,50 @@
     grad = (cotangent[...].astype(F32) * sigma * (1.0 + linear * (1.0 - sigma))).astype(BF)
     spread = (dot(neigh_weight[...], grad, ((1,), (1,))) * inverse).astype(BF)
     base[...] = dot(self_weight[...], grad, ((1,), (1,)))
+    column[...] = spread
     for i, left in enumerate((feats, mixed)):
         value = dot(left, grad, ((0,), (0,))).astype(BF)
-        for j in range(NZ // 2):
-            at = i * (NZ // 2) + j
-            payload[at, pl.ds(0, B)] = spread
-            payload[at, pl.ds(B, WG)] = value[j * WG : (j + 1) * WG]
+        for j in range(NY // 2):
+            grads[i * (NY // 2) + j] = value[j * WG : (j + 1) * WG]
 
 
 def dense_layer(pieces, features, cotangent, self_weight, neigh_weight, degrees):
     return pl.pallas_call(
         dense_kernel,
         in_specs=[VMEM] * 6,
-        out_specs=[VMEM] * 3,
+        out_specs=[VMEM] * 4,
         out_shape=[
             jax.ShapeDtypeStruct((B, F), BF),
             jax.ShapeDtypeStruct((F, B), F32),
-            jax.ShapeDtypeStruct((NZ, F + WG, B), BF),
+            jax.ShapeDtypeStruct((F, B), BF),
+            jax.ShapeDtypeStruct((NY, WG, F), BF),
         ],
         compiler_params=PARAMS,
         cost_estimate=cost(1.1),
         name="dense_layer",
     )(pieces, features, cotangent, self_weight, neigh_weight, degrees)
+
+
+def pack_kernel(column, grads, payload):
+    total = grads[0].astype(F32)
+    for i in range(1, NY):
+        total += grads[i].astype(F32)
+    chunk = total.astype(BF)
+    for i in range(NZ):
+        payload[i, pl.ds(0, F)] = column[...]
+        payload[i, pl.ds(F, WG)] = chunk
+
+
+def pack(column, grads):
+    return pl.pallas_call(
+        pack_kernel,
+        in_specs=[VMEM, VMEM],
+        out_specs=VMEM,
+        out_shape=jax.ShapeDtypeStruct((NZ, F + WG, B), BF),
+        compiler_params=PARAMS,
+        cost_estimate=cost(0.3),
+        name="pack",
+    )(column, grads)
 
 
 def relay_kernel(arrived, payload):
@@ -142,7 +165,7 @@
     )(arrived)
 
 
-def backward_kernel(plan, bits, spread, own, other, acc):
+def backward_kernel(plan, bits, spread, payload, acc):
     acc[...] = jnp.zeros_like(acc)
 
     slots = bits.shape[0]
@@ -153,77 +176,72 @@
         products.append(dot(block, bits[k]))
     for k in range(slots):
         acc[plan[2, k]] += products[k]
-    total = spread[0, pl.ds(NZ * F, WG)].astype(F32)
+    tail = spread[0, pl.ds(NZ * F, WG)].astype(F32)
     for i in range(1, NX):
-        total += spread[i, pl.ds(NZ * F, WG)].astype(F32)
-    chunk = total.astype(BF)
-    me = plan[4, 0]
+        tail += spread[i, pl.ds(NZ * F, WG)].astype(F32)
     for i in range(NY):
-        own[pl.ds(i * F, F)] = acc[me * NY + i].astype(BF)
-        other[pl.ds(i * F, F)] = acc[(1 - me) * NY + i].astype(BF)
-    own[pl.ds(NY * F, WG)] = chunk
-    other[pl.ds(NY * F, WG)] = chunk
+        for j in range(NC):
+            payload[i, pl.ds(j * F, F)] = acc[j * NY + i].astype(BF)
+        payload[i, pl.ds(NC * F, WG)] = tail.astype(BF)
 
 
 def backward_sums(plan, bits, spread):
     return pl.pallas_call(
         backward_kernel,
         in_specs=[SMEM, VMEM, VMEM],
-        out_specs=[VMEM, VMEM],
-        out_shape=[jax.ShapeDtypeStruct((NY * F + WG, B), BF)] * 2,
+        out_specs=VMEM,
+        out_shape=jax.ShapeDtypeStruct((NY, NC * F + WG, B), BF),
         scratch_shapes=[pltpu.VMEM((NY * NC + 1, F, B), F32)],
         compiler_params=PARAMS,
-        cost_estimate=cost(2.6),
+        cost_estimate=cost(1.5),
         name="backward_sums",
     )(plan, bits, spread)
 
 
-def merge_kernel(core, own, other, payload):
-    them = 1 - core[0]
-    tail = own[pl.ds(NY * F, WG)].astype(F32) + other[them, pl.ds(NY * F, WG)].astype(F32)
+def collect_kernel(arrived, sums):
+    total = arrived[0, pl.ds(0, NC * F)].astype(F32)
+    for i in range(1, NY):
+        total += arrived[i, pl.ds(0, NC * F)].astype(F32)
+    sums[pl.ds(0, NC * F)] = total.astype(BF)
     for i in range(NY):
-        at = pl.ds(i * F, F)
-        payload[i, pl.ds(0, F)] = (own[at].astype(F32) + other[them, at].astype(F32)).astype(BF)
-        payload[i, pl.ds(F, WG)] = tail.astype(BF)
-
-
-def merge(core, own, other):
-    return pl.pallas_call(
-        merge_kernel,
+        sums[pl.ds(NC * F + i * WG, WG)] = arrived[i, pl.ds(NC * F, WG)]
+
+
+def collect(arrived):
+    return pl.pallas_call(
+        collect_kernel,
+        in_specs=[VMEM],
+        out_specs=VMEM,
+        out_shape=jax.ShapeDtypeStruct((2 * NC * F, B), BF),
+        compiler_params=PARAMS,
+        cost_estimate=cost(0.3),
+        name="collect",
+    )(arrived)
+
+
+def final_kernel(core, both, base, grad_features, grad_self, grad_neigh):
+    mine = pl.ds(pl.multiple_of(core[0] * F, F), F)
+    total = base[...] + (both[0, mine].astype(F32) + both[1, mine].astype(F32))
+    grad_features[...] = total.T.astype(BF)
+    for i, out in ((NC, grad_self), (NC + 1, grad_neigh)):
+        rows = pl.ds(i * F, F)
+        out[...] = both[0, rows].astype(F32) + both[1, rows].astype(F32)
+
+
+def final(core, both, base):
+    return pl.pallas_call(
+        final_kernel,
         in_specs=[SMEM, VMEM, VMEM],
-        out_specs=VMEM,
-        out_shape=jax.ShapeDtypeStruct((NY, F + WG, B), BF),
-        compiler_params=PARAMS,
-        cost_estimate=cost(0.5),
-        name="merge",
-    )(core, own, other)
-
-
-def final_kernel(arrived, base, grad_features, chunk):
-    total = base[...]
-    tail = arrived[0, pl.ds(F, WG)].astype(F32)
-    for i in range(NY):
-        total += arrived[i, pl.ds(0, F)].astype(F32)
-        if i > 0:
-            tail += arrived[i, pl.ds(F, WG)].astype(F32)
-    grad_features[...] = total.T.astype(BF)
-    for i in range(NZ):
-        chunk[i] = tail.astype(BF)
-
-
-def final(arrived, base):
-    return pl.pallas_call(
-        final_kernel,
-        in_specs=[VMEM, VMEM],
-        out_specs=[VMEM, VMEM],
+        out_specs=[VMEM] * 3,
         out_shape=[
             jax.ShapeDtypeStruct((B, F), BF),
-            jax.ShapeDtypeStruct((NZ, WG, F), BF),
+            jax.ShapeDtypeStruct((F, F), F32),
+            jax.ShapeDtypeStruct((F, F), F32),
         ],
         compiler_params=PARAMS,
         cost_estimate=cost(0.8),
         name="final",
-    )(arrived, base)
+    )(core, both, base)
 
 
 def exchange(value, axis):
@@ -265,16 +283,14 @@
     partial = forward_sums(plan, bits, source)
     arrived = exchange(partial.reshape(NX, NZ, B, F), "x")
     pieces = exchange(add_pieces(arrived), "z")
-    hidden, base, payload = dense_layer(
+    hidden, base, column, grads = dense_layer(
         pieces, features, cotangent, self_weight, neigh_weight, degrees.reshape(1, B)
     )
+    payload = pack(column, exchange(grads, "y"))
     spread = exchange(relay(exchange(payload, "z")), "x")
-    own, other = backward_sums(plan, bits, spread)
-    other = lax.all_gather(other, "core", axis=0, tiled=False)
-    returned = exchange(merge(core.reshape(1), own, other), "y")
-    grad_features, chunk = final(returned, base)
-    grads = exchange(chunk, "z").reshape(2, F, F).astype(F32)
-    return (hidden, grad_features, grads[0], grads[1])
+    returned = exchange(backward_sums(plan, bits, spread), "y")
+    both = lax.all_gather(collect(returned), "core", axis=0, tiled=False)
+    return (hidden, *final(core.reshape(1), both, base))
 
 
 def solution(mesh):

time: 127 us -> 127 us (level)
    all_gather x1, blocking collectives: 7.43 us -> 9.54 us  [body(): both = lax.all_gather(collect(returned), 'core', axis=0, tiled=False)]
    all_to_all x6, blocking collectives: 88.4 us -> 86.8 us  [exchange(): return lax.all_to_all(value, axis, 0, 0, tiled=True)]
    pallas_call x4 -> x5, Pallas kernels: 3.2 us -> 3.26 us  [the longest x1 1.53 us: backward_sums(): pl.pallas_call(backward_kernel, in_specs=[SMEM, VMEM, VMEM], out_specs=VM...]
where the time goes in v3:
time: 127 us; the launch traced here: 126 us
  blocking collectives  102 us (80%)
  starting transfers between devices  7.65 us (6%)
  waiting for transfers between devices  5.35 us (4%)
  Pallas kernels  5.17 us (4%)
  other arithmetic  3.36 us (3%)
  local copies, waits for them, and re-layouts  1.55 us (1%)
  between operations  1.4 us (1%)
    all_to_all x6, blocking collectives, exchange(): return lax.all_to_all(value, axis, 0, 0, tiled=True)  86.8 us
    all_gather x1, blocking collectives, body(): both = lax.all_gather(collect(returned), 'core', axis=0, tiled=False)  9.54 us
    all_to_all x1, starting transfers between devices, exchange(): return lax.all_to_all(value, axis, 0, 0, tiled=True)  7.65 us
    all_gather x1, blocking collectives, body(): source = lax.all_gather(near, 'core', axis=0, tiled=True)  5.43 us
    all_to_all x1, waiting for transfers between devices, exchange(): return lax.all_to_all(value, axis, 0, 0, tiled=True)  5.35 us
    convert_element_type x1, other arithmetic, body(): bits = adjacency.reshape(slots, B, B).astype(BF)  2.67 us
  transfers between devices with their start and end apart: 1, of which 1 were waited for; matrix products, arithmetic and copies ran while one was open for 3% of the time, Pallas kernels for 0%

profile of v3, /device:TPU:1, one launch (start us, length us, event | category | flops | bytes accessed | tf_op | source)
XLA Modules:
  0.0 126.3 jit_solution(13485715515337228749)
XLA Ops:
  0.6 1.5 %broadcast_in_dim.12 = bf16[8,128,128]{2,1,0:T(8,128)(2,1)} broadcast(bf16[128,128]{1,0:T(8,128)(2,1)} %features.1), dimensions={1,2} | broadcast | bytes 294912 | tf_op jit(solution)/shard_map/broadcast_in_dim | solution.py:281
  2.1 7.7 %all-to-all-start = ((bf16[8,128,128]{2,1,0:T(8,128)(2,1)}), bf16[8,128,128]{2,1,0:T(8,128)(2,1)S(1)}, u32[]{:S(2)}, u32[]{:S(2)}) async-start(bf16[8,128,128]{2,1,0:T(8,128)(2,1)} %broadcast_in_dim.12), calls=%async_computation | async-start | bytes 524288 | tf_op jit(solution)/shard_map/all_to_all | solution.py:248
  10.4 0.7 compare_select_fusion.6
  11.2 2.7 %convert_bitcast_fusion.bits = bf16[64,128,128]{2,1,0:T(8,128)(2,1)S(1)} fusion(s32[1,1,64,128,128]{4,3,2,1,0:T(8,128)} %param.14), kind=kLoop, calls=%fused_computation | loop fusion | flops 1048576 | bytes 6291456 | tf_op jit(solution)/shard_map/convert_element_type | solution.py:279
  13.8 5.3 %all-to-all-done = bf16[8,128,128]{2,1,0:T(8,128)(2,1)S(1)} async-done(((bf16[8,128,128]{2,1,0:T(8,128)(2,1)}), bf16[8,128,128]{2,1,0:T(8,128)(2,1)S(1)}, u32[]{:S(2)}, u32[]{:S(2)}) %all-to-all-start) | async-done | bytes 262176 | tf_op jit(solution)/shard_map/all_to_all | solution.py:248
  19.2 5.4 %all_gather.9.source = bf16[16,128,128]{2,1,0:T(8,128)(2,1)S(1)} all-gather(bf16[8,128,128]{2,1,0:T(8,128)(2,1)S(1)} %all-to-all-done), channel_id=1, replica_groups=mesh['z'=8,'x'=4,'y'=8,'core'=2] {'core'}, dimensions={0}, use_global_device_ids=true | all-gather | bytes 786432 | tf_op jit(solution)/shard_map/all_gather | solution.py:282
  24.6 1.6 %forward_sums.1 = bf16[32,128,128]{2,1,0:T(8,128)(2,1)S(1)} custom-call(s32[5,64]{1,0:T(8,128)S(1)} %stack.2.plan, bf16[64,128,128]{2,1,0:T(8,128)(2,1)S(1)} %convert_bitcast_fusion.bits, bf16[16,128,128]{2,1,0:T(8,128)(2,1)S(1)} %all_gather.9.source), custom_call_target="tpu_custom_call" | custom-call | bytes 9963000 | tf_op jit(solution)/shard_map/forward_sums/pallas_call | solution.py:44
  26.3 0.0 copy-start
  26.3 0.0 copy-start.1
  26.3 0.0 copy-start.2
  26.3 0.0 copy-start.3
  26.3 0.0 copy-start.4
  26.3 18.0 %all_to_all.35.arrived = bf16[4,8,128,128]{3,2,1,0:T(8,128)(2,1)S(1)} all-to-all(bf16[4,8,128,128]{3,2,1,0:T(8,128)(2,1)S(1)} %bitcast.36), channel_id=1, replica_groups=mesh['z'=8,'x'=4,'y'=8,'core'=2] {'x'}, dimensions={0} | all-to-all | bytes 2097152 | tf_op jit(solution)/shard_map/all_to_all | solution.py:248
  44.3 0.1 add_pieces.1
  44.4 19.1 %all_to_all.36.pieces = bf16[8,128,128]{2,1,0:T(8,128)(2,1)S(1)} all-to-all(bf16[8,128,128]{2,1,0:T(8,128)(2,1)S(1)} %add_pieces.1), channel_id=1, replica_groups=mesh['z'=8,'x'=4,'y'=8,'core'=2] {'z'}, dimensions={0} | all-to-all | bytes 524288 | tf_op jit(solution)/shard_map/all_to_all | solution.py:248
  63.5 0.0 copy-done
  63.5 0.0 copy-done.1
  63.5 0.0 copy-done.2
  63.5 0.0 copy-done.3
  63.5 0.0 copy-done.4
  63.5 0.9 dense_layer.1
  64.4 9.6 %all_to_all.37.grads = bf16[8,32,128]{2,1,0:T(8,128)(2,1)S(1)} all-to-all(bf16[8,32,128]{2,1,0:T(8,128)(2,1)S(1)} %get-tuple-element.13), channel_id=1, replica_groups=mesh['z'=8,'x'=4,'y'=8,'core'=2] {'y'}, dimensions={0} | all-to-all | bytes 131072 | tf_op jit(solution)/shard_map/all_to_all | solution.py:248
  74.1 12.6 %all_to_all.38.arrived = bf16[8,160,128]{2,1,0:T(8,128)(2,1)S(1)} all-to-all(bf16[8,160,128]{2,1,0:T(8,128)(2,1)S(1)} %pack.1), channel_id=1, replica_groups=mesh['z'=8,'x'=4,'y'=8,'core'=2] {'z'}, dimensions={0} | all-to-all | bytes 655360 | tf_op jit(solution)/shard_map/all_to_all | solution.py:248
  86.6 0.1 relay.1
  86.8 12.3 %all_to_all.39.spread = bf16[4,1056,128]{2,1,0:T(8,128)(2,1)S(1)} all-to-all(bf16[4,1056,128]{2,1,0:T(8,128)(2,1)S(1)} %relay.1), channel_id=1, replica_groups=mesh['z'=8,'x'=4,'y'=8,'core'=2] {'x'}, dimensions={0} | all-to-all | bytes 2162688 | tf_op jit(solution)/shard_map/all_to_all | solution.py:248
  99.1 1.5 %backward_sums.1 = bf16[8,288,128]{2,1,0:T(8,128)(2,1)S(1)} custom-call(s32[5,64]{1,0:T(8,128)S(1)} %stack.2.plan, bf16[64,128,128]{2,1,0:T(8,128)(2,1)S(1)} %convert_bitcast_fusion.bits, bf16[4,1056,128]{2,1,0:T(8,128)(2,1)S(1)} %all_to_all.39.spread), custom_call_target="tpu_custom_call" | custom-call | bytes 5535000 | tf_op jit(solution)/shard_map/backward_sums/pallas_call | solution.py:189
  100.6 15.3 %all_to_all.40.arrived = bf16[8,288,128]{2,1,0:T(8,128)(2,1)S(1)} all-to-all(bf16[8,288,128]{2,1,0:T(8,128)(2,1)S(1)} %backward_sums.1), channel_id=1, replica_groups=mesh['z'=8,'x'=4,'y'=8,'core'=2] {'y'}, dimensions={0} | all-to-all | bytes 1179648 | tf_op jit(solution)/shard_map/all_to_all | solution.py:248
  116.0 0.1 collect.1
  116.0 9.5 %all-gather = bf16[1024,128]{1,0:T(8,128)(2,1)S(1)} all-gather(bf16[512,128]{1,0:T(8,128)(2,1)S(1)} %collect.1), channel_id=2, replica_groups=mesh['z'=8,'x'=4,'y'=8,'core'=2] {'core'}, dimensions={0}, use_global_device_ids=true | all-gather | bytes 393216 | tf_op jit(solution)/shard_map/all_gather | solution.py:292
  125.6 0.7 final.1
  (3 shorter events, 0.1 us)
Async XLA Ops:
  2.1 17.1 %all-to-all-start = ((bf16[8,128,128]{2,1,0:T(8,128)(2,1)}), bf16[8,128,128]{2,1,0:T(8,128)(2,1)S(1)}, u32[]{:S(2)}, u32[]{:S(2)}) async-start(bf16[8,128,128]{2,1,0:T(8,128)(2,1)} %broadcast_in_dim.12), calls=%async_computation | async-start | bytes 524288 | tf_op jit(solution)/shard_map/all_to_all | solution.py:248
  26.3 37.2 %copy-start = (bf16[128,128]{1,0:T(8,128)(2,1)S(1)}, bf16[128,128]{1,0:T(8,128)(2,1)}, u32[]{:S(2)}) copy-start(bf16[128,128]{1,0:T(8,128)(2,1)} %features.1) | copy-start | bytes 98308
  26.3 37.2 %copy-start.1 = (bf16[128,128]{1,0:T(8,128)(2,1)S(1)}, bf16[128,128]{1,0:T(8,128)(2,1)}, u32[]{:S(2)}) copy-start(bf16[128,128]{1,0:T(8,128)(2,1)} %cotangent.1) | copy-start | bytes 98308
  26.3 37.2 %copy-start.2 = (bf16[128,128]{1,0:T(8,128)(2,1)S(1)}, bf16[128,128]{1,0:T(8,128)(2,1)}, u32[]{:S(2)}) copy-start(bf16[128,128]{1,0:T(8,128)(2,1)} %self_weight.1) | copy-start | bytes 98308
  26.3 37.2 %copy-start.3 = (bf16[128,128]{1,0:T(8,128)(2,1)S(1)}, bf16[128,128]{1,0:T(8,128)(2,1)}, u32[]{:S(2)}) copy-start(bf16[128,128]{1,0:T(8,128)(2,1)} %neigh_weight.1) | copy-start | bytes 98308
  26.3 37.2 %copy-start.4 = (s32[128]{0:T(128)S(1)}, s32[128]{0:T(128)}, u32[]{:S(2)}) copy-start(s32[128]{0:T(128)} %param.13) | copy-start | bytes 1540

commit v4 on v3

--- a/solution.py
+++ b/solution.py
@@ -22,6 +22,7 @@
 
 
 VMEM = pl.BlockSpec(memory_space=pltpu.VMEM)
+ANY = pl.BlockSpec(memory_space=pl.ANY)
 SMEM = pl.BlockSpec(memory_space=pltpu.SMEM)
 PARAMS = pltpu.CompilerParams(vmem_limit_bytes=24 * 1024 * 1024)
 
@@ -30,8 +31,11 @@
     return lax.dot_general(a, b, (contract, ((), ())), preferred_element_type=F32)
 
 
-def forward_kernel(plan, bits, source, partial, acc):
+def forward_kernel(whole, bits, source, partial, acc, plan, sem):
+    copy = pltpu.make_async_copy(whole, plan, sem)
+    copy.start()
     acc[...] = jnp.zeros_like(acc)
+    copy.wait()
 
     slots = bits.shape[0]
     products = [dot(bits[k], source[plan[0, k]]) for k in range(slots)]
@@ -43,10 +47,14 @@
 def forward_sums(plan, bits, source):
     return pl.pallas_call(
         forward_kernel,
-        in_specs=[SMEM, VMEM, VMEM],
+        in_specs=[ANY, VMEM, VMEM],
         out_specs=VMEM,
         out_shape=jax.ShapeDtypeStruct((NX * NZ, B, F), BF),
-        scratch_shapes=[pltpu.VMEM((NX * NZ + 1, B, F), F32)],
+        scratch_shapes=[
+            pltpu.VMEM((NX * NZ + 1, B, F), F32),
+            pltpu.SMEM(plan.shape, jnp.int32),
+            pltpu.SemaphoreType.DMA,
+        ],
         compiler_params=PARAMS,
         cost_estimate=cost(2.7),
         name="forward_sums",
@@ -165,8 +173,11 @@
     )(arrived)
 
 
-def backward_kernel(plan, bits, spread, payload, acc):
+def backward_kernel(whole, bits, spread, payload, acc, plan, sem):
+    copy = pltpu.make_async_copy(whole, plan, sem)
+    copy.start()
     acc[...] = jnp.zeros_like(acc)
+    copy.wait()
 
     slots = bits.shape[0]
     products = []
@@ -188,10 +199,14 @@
 def backward_sums(plan, bits, spread):
     return pl.pallas_call(
         backward_kernel,
-        in_specs=[SMEM, VMEM, VMEM],
+        in_specs=[ANY, VMEM, VMEM],
         out_specs=VMEM,
         out_shape=jax.ShapeDtypeStruct((NY, NC * F + WG, B), BF),
-        scratch_shapes=[pltpu.VMEM((NY * NC + 1, F, B), F32)],
+        scratch_shapes=[
+            pltpu.VMEM((NY * NC + 1, F, B), F32),
+            pltpu.SMEM(plan.shape, jnp.int32),
+            pltpu.SemaphoreType.DMA,
+        ],
         compiler_params=PARAMS,
         cost_estimate=cost(1.5),
         name="backward_sums",
@@ -219,7 +234,8 @@
     )(arrived)
 
 
-def final_kernel(core, both, base, grad_features, grad_self, grad_neigh):
+def final_kernel(core, both, base, activated, hidden, grad_features, grad_self, grad_neigh):
+    hidden[...] = activated[...]
     mine = pl.ds(pl.multiple_of(core[0] * F, F), F)
     total = base[...] + (both[0, mine].astype(F32) + both[1, mine].astype(F32))
     grad_features[...] = total.T.astype(BF)
@@ -228,12 +244,13 @@
         out[...] = both[0, rows].astype(F32) + both[1, rows].astype(F32)
 
 
-def final(core, both, base):
+def final(core, both, base, activated):
     return pl.pallas_call(
         final_kernel,
-        in_specs=[SMEM, VMEM, VMEM],
-        out_specs=[VMEM] * 3,
+        in_specs=[SMEM, VMEM, VMEM, VMEM],
+        out_specs=[VMEM] * 4,
         out_shape=[
+            jax.ShapeDtypeStruct((B, F), BF),
             jax.ShapeDtypeStruct((B, F), BF),
             jax.ShapeDtypeStruct((F, F), F32),
             jax.ShapeDtypeStruct((F, F), F32),
@@ -241,7 +258,7 @@
         compiler_params=PARAMS,
         cost_estimate=cost(0.8),
         name="final",
-    )(core, both, base)
+    )(core, both, base, activated)
 
 
 def exchange(value, axis):
@@ -283,14 +300,14 @@
     partial = forward_sums(plan, bits, source)
     arrived = exchange(partial.reshape(NX, NZ, B, F), "x")
     pieces = exchange(add_pieces(arrived), "z")
-    hidden, base, column, grads = dense_layer(
+    activated, base, column, grads = dense_layer(
         pieces, features, cotangent, self_weight, neigh_weight, degrees.reshape(1, B)
     )
     payload = pack(column, exchange(grads, "y"))
     spread = exchange(relay(exchange(payload, "z")), "x")
     returned = exchange(backward_sums(plan, bits, spread), "y")
     both = lax.all_gather(collect(returned), "core", axis=0, tiled=False)
-    return (hidden, *final(core.reshape(1), both, base))
+    return tuple(final(core.reshape(1), both, base, activated))
 
 
 def solution(mesh):

time: 127 us -> 126 us (level)
  no operation moved by 1% of the time
where the time goes in v4:
time: 126 us
  blocking collectives  102 us (81%)
  starting transfers between devices  7.65 us (6%)
  waiting for transfers between devices  5.35 us (4%)
  Pallas kernels  4.65 us (4%)
  other arithmetic  3.36 us (3%)
  local copies, waits for them, and re-layouts  1.55 us (1%)
  between operations  1.4 us (1%)
    all_to_all x6, blocking collectives, exchange(): return lax.all_to_all(value, axis, 0, 0, tiled=True)  86.9 us
    all_gather x1, blocking collectives, body(): both = lax.all_gather(collect(returned), 'core', axis=0, tiled=False)  9.52 us
    all_to_all x1, starting transfers between devices, exchange(): return lax.all_to_all(value, axis, 0, 0, tiled=True)  7.65 us
    all_gather x1, blocking collectives, body(): source = lax.all_gather(near, 'core', axis=0, tiled=True)  5.43 us
    all_to_all x1, waiting for transfers between devices, exchange(): return lax.all_to_all(value, axis, 0, 0, tiled=True)  5.35 us
    convert_element_type x1, other arithmetic, body(): bits = adjacency.reshape(slots, B, B).astype(BF)  2.67 us
  transfers between devices with their start and end apart: 1, of which 1 were waited for; matrix products, arithmetic and copies ran while one was open for 3% of the time, Pallas kernels for 0%

profile of v4, /device:TPU:1, one launch (start us, length us, event | category | flops | bytes accessed | tf_op | source)
XLA Modules:
  0.0 125.8 jit_solution(8397661929816223601)
XLA Ops:
  0.6 1.5 %broadcast_in_dim.12 = bf16[8,128,128]{2,1,0:T(8,128)(2,1)} broadcast(bf16[128,128]{1,0:T(8,128)(2,1)} %features.1), dimensions={1,2} | broadcast | bytes 294912 | tf_op jit(solution)/shard_map/broadcast_in_dim | solution.py:298
  2.1 7.7 %all-to-all-start = ((bf16[8,128,128]{2,1,0:T(8,128)(2,1)}), bf16[8,128,128]{2,1,0:T(8,128)(2,1)S(1)}, u32[]{:S(2)}, u32[]{:S(2)}) async-start(bf16[8,128,128]{2,1,0:T(8,128)(2,1)} %broadcast_in_dim.12), calls=%async_computation | async-start | bytes 524288 | tf_op jit(solution)/shard_map/all_to_all | solution.py:265
  10.4 0.7 compare_select_fusion.6
  11.2 2.7 %convert_bitcast_fusion.bits = bf16[64,128,128]{2,1,0:T(8,128)(2,1)S(1)} fusion(s32[1,1,64,128,128]{4,3,2,1,0:T(8,128)} %param.14), kind=kLoop, calls=%fused_computation | loop fusion | flops 1048576 | bytes 6291456 | tf_op jit(solution)/shard_map/convert_element_type | solution.py:296
  13.8 5.3 %all-to-all-done = bf16[8,128,128]{2,1,0:T(8,128)(2,1)S(1)} async-done(((bf16[8,128,128]{2,1,0:T(8,128)(2,1)}), bf16[8,128,128]{2,1,0:T(8,128)(2,1)S(1)}, u32[]{:S(2)}, u32[]{:S(2)}) %all-to-all-start) | async-done | bytes 262176 | tf_op jit(solution)/shard_map/all_to_all | solution.py:265
  19.2 5.4 %all_gather.9.source = bf16[16,128,128]{2,1,0:T(8,128)(2,1)S(1)} all-gather(bf16[8,128,128]{2,1,0:T(8,128)(2,1)S(1)} %all-to-all-done), channel_id=1, replica_groups=mesh['z'=8,'x'=4,'y'=8,'core'=2] {'core'}, dimensions={0}, use_global_device_ids=true | all-gather | bytes 786432 | tf_op jit(solution)/shard_map/all_gather | solution.py:299
  24.6 1.5 %forward_sums.1 = bf16[32,128,128]{2,1,0:T(8,128)(2,1)S(1)} custom-call(s32[5,64]{1,0:T(8,128)S(1)} %stack.2.whole, bf16[64,128,128]{2,1,0:T(8,128)(2,1)S(1)} %convert_bitcast_fusion.bits, bf16[16,128,128]{2,1,0:T(8,128)(2,1)S(1)} %all_gather.9.source), custom_call_target="tpu_custom_call" | custom-call | bytes 9963000 | tf_op jit(solution)/shard_map/forward_sums/pallas_call | solution.py:48
  26.2 0.0 copy-start
  26.2 0.0 copy-start.1
  26.2 0.0 copy-start.2
  26.2 0.0 copy-start.3
  26.2 0.0 copy-start.4
  26.2 18.0 %all_to_all.35.arrived = bf16[4,8,128,128]{3,2,1,0:T(8,128)(2,1)S(1)} all-to-all(bf16[4,8,128,128]{3,2,1,0:T(8,128)(2,1)S(1)} %bitcast.36), channel_id=1, replica_groups=mesh['z'=8,'x'=4,'y'=8,'core'=2] {'x'}, dimensions={0} | all-to-all | bytes 2097152 | tf_op jit(solution)/shard_map/all_to_all | solution.py:265
  44.2 0.1 add_pieces.1
  44.3 19.1 %all_to_all.36.pieces = bf16[8,128,128]{2,1,0:T(8,128)(2,1)S(1)} all-to-all(bf16[8,128,128]{2,1,0:T(8,128)(2,1)S(1)} %add_pieces.1), channel_id=1, replica_groups=mesh['z'=8,'x'=4,'y'=8,'core'=2] {'z'}, dimensions={0} | all-to-all | bytes 524288 | tf_op jit(solution)/shard_map/all_to_all | solution.py:265
  63.4 0.0 copy-done
  63.4 0.0 copy-done.1
  63.4 0.0 copy-done.2
  63.4 0.0 copy-done.3
  63.4 0.0 copy-done.4
  63.4 0.4 dense_layer.1
  63.9 9.6 %all_to_all.37.grads = bf16[8,32,128]{2,1,0:T(8,128)(2,1)S(1)} all-to-all(bf16[8,32,128]{2,1,0:T(8,128)(2,1)S(1)} %get-tuple-element.9), channel_id=1, replica_groups=mesh['z'=8,'x'=4,'y'=8,'core'=2] {'y'}, dimensions={0} | all-to-all | bytes 131072 | tf_op jit(solution)/shard_map/all_to_all | solution.py:265
  73.5 12.6 %all_to_all.38.arrived = bf16[8,160,128]{2,1,0:T(8,128)(2,1)S(1)} all-to-all(bf16[8,160,128]{2,1,0:T(8,128)(2,1)S(1)} %pack.1), channel_id=1, replica_groups=mesh['z'=8,'x'=4,'y'=8,'core'=2] {'z'}, dimensions={0} | all-to-all | bytes 655360 | tf_op jit(solution)/shard_map/all_to_all | solution.py:265
  86.1 0.1 relay.1
  86.3 12.3 %all_to_all.39.spread = bf16[4,1056,128]{2,1,0:T(8,128)(2,1)S(1)} all-to-all(bf16[4,1056,128]{2,1,0:T(8,128)(2,1)S(1)} %relay.1), channel_id=1, replica_groups=mesh['z'=8,'x'=4,'y'=8,'core'=2] {'x'}, dimensions={0} | all-to-all | bytes 2162688 | tf_op jit(solution)/shard_map/all_to_all | solution.py:265
  98.6 1.5 %backward_sums.1 = bf16[8,288,128]{2,1,0:T(8,128)(2,1)S(1)} custom-call(s32[5,64]{1,0:T(8,128)S(1)} %stack.2.whole, bf16[64,128,128]{2,1,0:T(8,128)(2,1)S(1)} %convert_bitcast_fusion.bits, bf16[4,1056,128]{2,1,0:T(8,128)(2,1)S(1)} %all_to_all.39.spread), custom_call_target="tpu_custom_call" | custom-call | bytes 5535000 | tf_op jit(solution)/shard_map/backward_sums/pallas_call | solution.py:200
  100.1 15.3 %all_to_all.40.arrived = bf16[8,288,128]{2,1,0:T(8,128)(2,1)S(1)} all-to-all(bf16[8,288,128]{2,1,0:T(8,128)(2,1)S(1)} %backward_sums.1), channel_id=1, replica_groups=mesh['z'=8,'x'=4,'y'=8,'core'=2] {'y'}, dimensions={0} | all-to-all | bytes 1179648 | tf_op jit(solution)/shard_map/all_to_all | solution.py:265
  115.5 0.1 collect.1
  115.6 9.5 %all-gather = bf16[1024,128]{1,0:T(8,128)(2,1)S(1)} all-gather(bf16[512,128]{1,0:T(8,128)(2,1)S(1)} %collect.1), channel_id=2, replica_groups=mesh['z'=8,'x'=4,'y'=8,'core'=2] {'core'}, dimensions={0}, use_global_device_ids=true | all-gather | bytes 393216 | tf_op jit(solution)/shard_map/all_gather | solution.py:309
  125.1 0.7 final.1
  (3 shorter events, 0.1 us)
Async XLA Ops:
  2.1 17.1 %all-to-all-start = ((bf16[8,128,128]{2,1,0:T(8,128)(2,1)}), bf16[8,128,128]{2,1,0:T(8,128)(2,1)S(1)}, u32[]{:S(2)}, u32[]{:S(2)}) async-start(bf16[8,128,128]{2,1,0:T(8,128)(2,1)} %broadcast_in_dim.12), calls=%async_computation | async-start | bytes 524288 | tf_op jit(solution)/shard_map/all_to_all | solution.py:265
  26.2 37.2 %copy-start = (bf16[128,128]{1,0:T(8,128)(2,1)S(1)}, bf16[128,128]{1,0:T(8,128)(2,1)}, u32[]{:S(2)}) copy-start(bf16[128,128]{1,0:T(8,128)(2,1)} %features.1) | copy-start | bytes 98308
  26.2 37.2 %copy-start.1 = (bf16[128,128]{1,0:T(8,128)(2,1)S(1)}, bf16[128,128]{1,0:T(8,128)(2,1)}, u32[]{:S(2)}) copy-start(bf16[128,128]{1,0:T(8,128)(2,1)} %cotangent.1) | copy-start | bytes 98308
  26.2 37.2 %copy-start.2 = (bf16[128,128]{1,0:T(8,128)(2,1)S(1)}, bf16[128,128]{1,0:T(8,128)(2,1)}, u32[]{:S(2)}) copy-start(bf16[128,128]{1,0:T(8,128)(2,1)} %self_weight.1) | copy-start | bytes 98308
  26.2 37.2 %copy-start.3 = (bf16[128,128]{1,0:T(8,128)(2,1)S(1)}, bf16[128,128]{1,0:T(8,128)(2,1)}, u32[]{:S(2)}) copy-start(bf16[128,128]{1,0:T(8,128)(2,1)} %neigh_weight.1) | copy-start | bytes 98308
  26.2 37.2 %copy-start.4 = (s32[128]{0:T(128)S(1)}, s32[128]{0:T(128)}, u32[]{:S(2)}) copy-start(s32[128]{0:T(128)} %param.13) | copy-start | bytes 1540

commit v5 on v4

--- a/solution.py
+++ b/solution.py
@@ -22,6 +22,7 @@
 
 
 VMEM = pl.BlockSpec(memory_space=pltpu.VMEM)
+HBM = pl.BlockSpec(memory_space=pltpu.HBM)
 ANY = pl.BlockSpec(memory_space=pl.ANY)
 SMEM = pl.BlockSpec(memory_space=pltpu.SMEM)
 PARAMS = pltpu.CompilerParams(vmem_limit_bytes=24 * 1024 * 1024)
@@ -261,6 +262,33 @@
     )(core, both, base, activated)
 
 
+def repeat_kernel(block, payload, held, sem, sems):
+    load = pltpu.make_async_copy(block, held, sem)
+    load.start()
+    load.wait()
+    copies = [pltpu.make_async_copy(held, payload.at[i], sems.at[i]) for i in range(NY)]
+    for copy in copies:
+        copy.start()
+    for copy in copies:
+        copy.wait()
+
+
+def repeat(block):
+    return pl.pallas_call(
+        repeat_kernel,
+        in_specs=[HBM],
+        out_specs=HBM,
+        out_shape=jax.ShapeDtypeStruct((NY, B, F), BF),
+        scratch_shapes=[
+            pltpu.VMEM((B, F), BF),
+            pltpu.SemaphoreType.DMA,
+            pltpu.SemaphoreType.DMA((NY,)),
+        ],
+        cost_estimate=cost(1.0),
+        name="repeat",
+    )(block)
+
+
 def exchange(value, axis):
     return lax.all_to_all(value, axis, 0, 0, tiled=True)
 
@@ -295,7 +323,7 @@
     )
     bits = adjacency.reshape(slots, B, B).astype(BF)
 
-    near = exchange(jnp.broadcast_to(features, (NY, B, F)), "y")
+    near = exchange(repeat(features), "y")
     source = lax.all_gather(near, "core", axis=0, tiled=True)
     partial = forward_sums(plan, bits, source)
     arrived = exchange(partial.reshape(NX, NZ, B, F), "x")

time: 126 us -> 126 us (level)
  Pallas kernels: 4.65 us -> 6.19 us
  local copies, waits for them, and re-layouts: 1.55 us -> 0.06 us
    pallas_call x0 -> x1, Pallas kernels: none -> 1.53 us  [repeat(): pl.pallas_call(repeat_kernel, in_specs=[HBM], out_specs=HBM, out_shape=ja...]
    broadcast_in_dim x1 -> x0, local copies, waits for them, and re-layouts: 1.49 us -> none  [body(): near = exchange(jnp.broadcast_to(features, (NY, B, F)), 'y')]
where the time goes in v5:
time: 126 us
  blocking collectives  102 us (81%)
  starting transfers between devices  7.66 us (6%)
  Pallas kernels  6.19 us (5%)
  waiting for transfers between devices  5.35 us (4%)
  other arithmetic  3.36 us (3%)
  between operations  1.41 us (1%)
    all_to_all x6, blocking collectives, exchange(): return lax.all_to_all(value, axis, 0, 0, tiled=True)  86.9 us
    all_gather x1, blocking collectives, body(): both = lax.all_gather(collect(returned), 'core', axis=0, tiled=False)  9.51 us
    all_to_all x1, starting transfers between devices, exchange(): return lax.all_to_all(value, axis, 0, 0, tiled=True)  7.66 us
    all_gather x1, blocking collectives, body(): source = lax.all_gather(near, 'core', axis=0, tiled=True)  5.43 us
    all_to_all x1, waiting for transfers between devices, exchange(): return lax.all_to_all(value, axis, 0, 0, tiled=True)  5.35 us
    convert_element_type x1, other arithmetic, body(): bits = adjacency.reshape(slots, B, B).astype(BF)  2.67 us
  transfers between devices with their start and end apart: 1, of which 1 were waited for; matrix products, arithmetic and copies ran while one was open for 3% of the time, Pallas kernels for 0%

profile of v5, /device:TPU:1, one launch (start us, length us, event | category | flops | bytes accessed | tf_op | source)
XLA Modules:
  0.0 125.9 jit_solution(3378461437895721823)
XLA Ops:
  0.6 1.5 %repeat.1 = bf16[8,128,128]{2,1,0:T(8,128)(2,1)} custom-call(bf16[128,128]{1,0:T(8,128)(2,1)} %features.1), custom_call_target="tpu_custom_call" | custom-call | bytes 3690000 | tf_op jit(solution)/shard_map/repeat/pallas_call | solution.py:277
  2.2 7.7 %all-to-all-start = ((bf16[8,128,128]{2,1,0:T(8,128)(2,1)}), bf16[8,128,128]{2,1,0:T(8,128)(2,1)S(1)}, u32[]{:S(2)}, u32[]{:S(2)}) async-start(bf16[8,128,128]{2,1,0:T(8,128)(2,1)} %repeat.1), calls=%async_computation | async-start | bytes 524288 | tf_op jit(solution)/shard_map/all_to_all | solution.py:293
  10.5 0.7 compare_select_fusion.6
  11.2 2.7 %convert_bitcast_fusion.bits = bf16[64,128,128]{2,1,0:T(8,128)(2,1)S(1)} fusion(s32[1,1,64,128,128]{4,3,2,1,0:T(8,128)} %param.14), kind=kLoop, calls=%fused_computation | loop fusion | flops 1048576 | bytes 6291456 | tf_op jit(solution)/shard_map/convert_element_type | solution.py:324
  13.9 5.3 %all-to-all-done = bf16[8,128,128]{2,1,0:T(8,128)(2,1)S(1)} async-done(((bf16[8,128,128]{2,1,0:T(8,128)(2,1)}), bf16[8,128,128]{2,1,0:T(8,128)(2,1)S(1)}, u32[]{:S(2)}, u32[]{:S(2)}) %all-to-all-start) | async-done | bytes 262176 | tf_op jit(solution)/shard_map/all_to_all | solution.py:293
  19.2 5.4 %all_gather.9.source = bf16[16,128,128]{2,1,0:T(8,128)(2,1)S(1)} all-gather(bf16[8,128,128]{2,1,0:T(8,128)(2,1)S(1)} %all-to-all-done), channel_id=1, replica_groups=mesh['z'=8,'x'=4,'y'=8,'core'=2] {'core'}, dimensions={0}, use_global_device_ids=true | all-gather | bytes 786432 | tf_op jit(solution)/shard_map/all_gather | solution.py:327
  24.7 1.5 %forward_sums.1 = bf16[32,128,128]{2,1,0:T(8,128)(2,1)S(1)} custom-call(s32[5,64]{1,0:T(8,128)S(1)} %stack.2.whole, bf16[64,128,128]{2,1,0:T(8,128)(2,1)S(1)} %convert_bitcast_fusion.bits, bf16[16,128,128]{2,1,0:T(8,128)(2,1)S(1)} %all_gather.9.source), custom_call_target="tpu_custom_call" | custom-call | bytes 9963000 | tf_op jit(solution)/shard_map/forward_sums/pallas_call | solution.py:49
  26.2 0.0 copy-start
  26.2 0.0 copy-start.1
  26.2 0.0 copy-start.2
  26.3 0.0 copy-start.3
  26.3 0.0 copy-start.4
  26.3 18.0 %all_to_all.35.arrived = bf16[4,8,128,128]{3,2,1,0:T(8,128)(2,1)S(1)} all-to-all(bf16[4,8,128,128]{3,2,1,0:T(8,128)(2,1)S(1)} %bitcast.36), channel_id=1, replica_groups=mesh['z'=8,'x'=4,'y'=8,'core'=2] {'x'}, dimensions={0} | all-to-all | bytes 2097152 | tf_op jit(solution)/shard_map/all_to_all | solution.py:293
  44.2 0.1 add_pieces.1
  44.4 19.1 %all_to_all.36.pieces = bf16[8,128,128]{2,1,0:T(8,128)(2,1)S(1)} all-to-all(bf16[8,128,128]{2,1,0:T(8,128)(2,1)S(1)} %add_pieces.1), channel_id=1, replica_groups=mesh['z'=8,'x'=4,'y'=8,'core'=2] {'z'}, dimensions={0} | all-to-all | bytes 524288 | tf_op jit(solution)/shard_map/all_to_all | solution.py:293
  63.4 0.0 copy-done
  63.4 0.0 copy-done.1
  63.4 0.0 copy-done.2
  63.5 0.0 copy-done.3
  63.5 0.0 copy-done.4
  63.5 0.4 dense_layer.1
  63.9 9.6 %all_to_all.37.grads = bf16[8,32,128]{2,1,0:T(8,128)(2,1)S(1)} all-to-all(bf16[8,32,128]{2,1,0:T(8,128)(2,1)S(1)} %get-tuple-element.9), channel_id=1, replica_groups=mesh['z'=8,'x'=4,'y'=8,'core'=2] {'y'}, dimensions={0} | all-to-all | bytes 131072 | tf_op jit(solution)/shard_map/all_to_all | solution.py:293
  73.6 12.6 %all_to_all.38.arrived = bf16[8,160,128]{2,1,0:T(8,128)(2,1)S(1)} all-to-all(bf16[8,160,128]{2,1,0:T(8,128)(2,1)S(1)} %pack.1), channel_id=1, replica_groups=mesh['z'=8,'x'=4,'y'=8,'core'=2] {'z'}, dimensions={0} | all-to-all | bytes 655360 | tf_op jit(solution)/shard_map/all_to_all | solution.py:293
  86.2 0.1 relay.1
  86.3 12.3 %all_to_all.39.spread = bf16[4,1056,128]{2,1,0:T(8,128)(2,1)S(1)} all-to-all(bf16[4,1056,128]{2,1,0:T(8,128)(2,1)S(1)} %relay.1), channel_id=1, replica_groups=mesh['z'=8,'x'=4,'y'=8,'core'=2] {'x'}, dimensions={0} | all-to-all | bytes 2162688 | tf_op jit(solution)/shard_map/all_to_all | solution.py:293
  98.7 1.5 %backward_sums.1 = bf16[8,288,128]{2,1,0:T(8,128)(2,1)S(1)} custom-call(s32[5,64]{1,0:T(8,128)S(1)} %stack.2.whole, bf16[64,128,128]{2,1,0:T(8,128)(2,1)S(1)} %convert_bitcast_fusion.bits, bf16[4,1056,128]{2,1,0:T(8,128)(2,1)S(1)} %all_to_all.39.spread), custom_call_target="tpu_custom_call" | custom-call | bytes 5535000 | tf_op jit(solution)/shard_map/backward_sums/pallas_call | solution.py:201
  100.2 15.3 %all_to_all.40.arrived = bf16[8,288,128]{2,1,0:T(8,128)(2,1)S(1)} all-to-all(bf16[8,288,128]{2,1,0:T(8,128)(2,1)S(1)} %backward_sums.1), channel_id=1, replica_groups=mesh['z'=8,'x'=4,'y'=8,'core'=2] {'y'}, dimensions={0} | all-to-all | bytes 1179648 | tf_op jit(solution)/shard_map/all_to_all | solution.py:293
  115.5 0.1 collect.1
  115.6 9.5 %all-gather = bf16[1024,128]{1,0:T(8,128)(2,1)S(1)} all-gather(bf16[512,128]{1,0:T(8,128)(2,1)S(1)} %collect.1), channel_id=2, replica_groups=mesh['z'=8,'x'=4,'y'=8,'core'=2] {'core'}, dimensions={0}, use_global_device_ids=true | all-gather | bytes 393216 | tf_op jit(solution)/shard_map/all_gather | solution.py:337
  125.1 0.7 final.1
  (3 shorter events, 0.1 us)
Async XLA Ops:
  2.2 17.1 %all-to-all-start = ((bf16[8,128,128]{2,1,0:T(8,128)(2,1)}), bf16[8,128,128]{2,1,0:T(8,128)(2,1)S(1)}, u32[]{:S(2)}, u32[]{:S(2)}) async-start(bf16[8,128,128]{2,1,0:T(8,128)(2,1)} %repeat.1), calls=%async_computation | async-start | bytes 524288 | tf_op jit(solution)/shard_map/all_to_all | solution.py:293
  26.2 37.2 %copy-start = (bf16[128,128]{1,0:T(8,128)(2,1)S(1)}, bf16[128,128]{1,0:T(8,128)(2,1)}, u32[]{:S(2)}) copy-start(bf16[128,128]{1,0:T(8,128)(2,1)} %features.1) | copy-start | bytes 98308
  26.2 37.2 %copy-start.1 = (bf16[128,128]{1,0:T(8,128)(2,1)S(1)}, bf16[128,128]{1,0:T(8,128)(2,1)}, u32[]{:S(2)}) copy-start(bf16[128,128]{1,0:T(8,128)(2,1)} %cotangent.1) | copy-start | bytes 98308
  26.2 37.2 %copy-start.2 = (bf16[128,128]{1,0:T(8,128)(2,1)S(1)}, bf16[128,128]{1,0:T(8,128)(2,1)}, u32[]{:S(2)}) copy-start(bf16[128,128]{1,0:T(8,128)(2,1)} %self_weight.1) | copy-start | bytes 98308
  26.3 37.2 %copy-start.3 = (bf16[128,128]{1,0:T(8,128)(2,1)S(1)}, bf16[128,128]{1,0:T(8,128)(2,1)}, u32[]{:S(2)}) copy-start(bf16[128,128]{1,0:T(8,128)(2,1)} %neigh_weight.1) | copy-start | bytes 98308
  26.3 37.2 %copy-start.4 = (s32[128]{0:T(128)S(1)}, s32[128]{0:T(128)}, u32[]{:S(2)}) copy-start(s32[128]{0:T(128)} %param.13) | copy-start | bytes 1540

commit v6 on v4

--- a/solution.py
+++ b/solution.py
@@ -213,33 +213,40 @@
     )(plan, bits, spread)
 
 
-def collect_kernel(arrived, sums):
-    total = arrived[0, pl.ds(0, NC * F)].astype(F32)
-    for i in range(1, NY):
-        total += arrived[i, pl.ds(0, NC * F)].astype(F32)
-    sums[pl.ds(0, NC * F)] = total.astype(BF)
+def collect_kernel(core, arrived, base, mine, packed):
+    def target(k):
+        rows = pl.ds(pl.multiple_of(k * F, F), F)
+        total = arrived[0, rows].astype(F32)
+        for i in range(1, NY):
+            total += arrived[i, rows].astype(F32)
+        return total
+
+    mine[...] = base[...] + target(core[0])
+    packed[pl.ds(0, F)] = target(1 - core[0]).astype(BF)
     for i in range(NY):
-        sums[pl.ds(NC * F + i * WG, WG)] = arrived[i, pl.ds(NC * F, WG)]
-
-
-def collect(arrived):
+        packed[pl.ds(F + i * WG, WG)] = arrived[i, pl.ds(NC * F, WG)]
+
+
+def collect(core, arrived, base):
     return pl.pallas_call(
         collect_kernel,
-        in_specs=[VMEM],
-        out_specs=VMEM,
-        out_shape=jax.ShapeDtypeStruct((2 * NC * F, B), BF),
+        in_specs=[SMEM, VMEM, VMEM],
+        out_specs=[VMEM, VMEM],
+        out_shape=[
+            jax.ShapeDtypeStruct((F, B), F32),
+            jax.ShapeDtypeStruct((F + NY * WG, B), BF),
+        ],
         compiler_params=PARAMS,
         cost_estimate=cost(0.3),
         name="collect",
-    )(arrived)
+    )(core, arrived, base)
 
 
 def final_kernel(core, both, base, activated, hidden, grad_features, grad_self, grad_neigh):
     hidden[...] = activated[...]
-    mine = pl.ds(pl.multiple_of(core[0] * F, F), F)
-    total = base[...] + (both[0, mine].astype(F32) + both[1, mine].astype(F32))
+    total = base[...] + both[1 - core[0], pl.ds(0, F)].astype(F32)
     grad_features[...] = total.T.astype(BF)
-    for i, out in ((NC, grad_self), (NC + 1, grad_neigh)):
+    for i, out in ((1, grad_self), (2, grad_neigh)):
         rows = pl.ds(i * F, F)
         out[...] = both[0, rows].astype(F32) + both[1, rows].astype(F32)
 
@@ -306,8 +313,10 @@
     payload = pack(column, exchange(grads, "y"))
     spread = exchange(relay(exchange(payload, "z")), "x")
     returned = exchange(backward_sums(plan, bits, spread), "y")
-    both = lax.all_gather(collect(returned), "core", axis=0, tiled=False)
-    return tuple(final(core.reshape(1), both, base, activated))
+    place = core.reshape(1)
+    mine, packed = collect(place, returned, base)
+    both = lax.all_gather(packed, "core", axis=0, tiled=False)
+    return tuple(final(place, both, mine, activated))
 
 
 def solution(mesh):

time: 126 us -> 126 us (level)
  no operation moved by 1% of the time
where the time goes in v6:
time: 126 us
  blocking collectives  102 us (81%)
  starting transfers between devices  7.65 us (6%)
  waiting for transfers between devices  5.35 us (4%)
  Pallas kernels  4.66 us (4%)
  other arithmetic  3.36 us (3%)
  local copies, waits for them, and re-layouts  1.55 us (1%)
  between operations  1.4 us (1%)
    all_to_all x6, blocking collectives, exchange(): return lax.all_to_all(value, axis, 0, 0, tiled=True)  86.9 us
    all_gather x1, blocking collectives, body(): both = lax.all_gather(packed, 'core', axis=0, tiled=False)  9.5 us
    all_to_all x1, starting transfers between devices, exchange(): return lax.all_to_all(value, axis, 0, 0, tiled=True)  7.65 us
    all_gather x1, blocking collectives, body(): source = lax.all_gather(near, 'core', axis=0, tiled=True)  5.43 us
    all_to_all x1, waiting for transfers between devices, exchange(): return lax.all_to_all(value, axis, 0, 0, tiled=True)  5.35 us
    convert_element_type x1, other arithmetic, body(): bits = adjacency.reshape(slots, B, B).astype(BF)  2.67 us
  transfers between devices with their start and end apart: 1, of which 1 were waited for; matrix products, arithmetic and copies ran while one was open for 3% of the time, Pallas kernels for 0%

profile of v6, /device:TPU:1, one launch (start us, length us, event | category | flops | bytes accessed | tf_op | source)
XLA Modules:
  0.0 125.8 jit_solution(682557030001008041)
XLA Ops:
  0.6 1.5 %broadcast_in_dim.12 = bf16[8,128,128]{2,1,0:T(8,128)(2,1)} broadcast(bf16[128,128]{1,0:T(8,128)(2,1)} %features.1), dimensions={1,2} | broadcast | bytes 294912 | tf_op jit(solution)/shard_map/broadcast_in_dim | solution.py:305
  2.1 7.7 %all-to-all-start = ((bf16[8,128,128]{2,1,0:T(8,128)(2,1)}), bf16[8,128,128]{2,1,0:T(8,128)(2,1)S(1)}, u32[]{:S(2)}, u32[]{:S(2)}) async-start(bf16[8,128,128]{2,1,0:T(8,128)(2,1)} %broadcast_in_dim.12), calls=%async_computation | async-start | bytes 524288 | tf_op jit(solution)/shard_map/all_to_all | solution.py:272
  10.4 0.7 compare_select_fusion.6
  11.2 2.7 %convert_bitcast_fusion.bits = bf16[64,128,128]{2,1,0:T(8,128)(2,1)S(1)} fusion(s32[1,1,64,128,128]{4,3,2,1,0:T(8,128)} %param.14), kind=kLoop, calls=%fused_computation | loop fusion | flops 1048576 | bytes 6291456 | tf_op jit(solution)/shard_map/convert_element_type | solution.py:303
  13.8 5.3 %all-to-all-done = bf16[8,128,128]{2,1,0:T(8,128)(2,1)S(1)} async-done(((bf16[8,128,128]{2,1,0:T(8,128)(2,1)}), bf16[8,128,128]{2,1,0:T(8,128)(2,1)S(1)}, u32[]{:S(2)}, u32[]{:S(2)}) %all-to-all-start) | async-done | bytes 262176 | tf_op jit(solution)/shard_map/all_to_all | solution.py:272
  19.2 5.4 %all_gather.9.source = bf16[16,128,128]{2,1,0:T(8,128)(2,1)S(1)} all-gather(bf16[8,128,128]{2,1,0:T(8,128)(2,1)S(1)} %all-to-all-done), channel_id=1, replica_groups=mesh['z'=8,'x'=4,'y'=8,'core'=2] {'core'}, dimensions={0}, use_global_device_ids=true | all-gather | bytes 786432 | tf_op jit(solution)/shard_map/all_gather | solution.py:306
  24.6 1.5 %forward_sums.1 = bf16[32,128,128]{2,1,0:T(8,128)(2,1)S(1)} custom-call(s32[5,64]{1,0:T(8,128)S(1)} %stack.2.whole, bf16[64,128,128]{2,1,0:T(8,128)(2,1)S(1)} %convert_bitcast_fusion.bits, bf16[16,128,128]{2,1,0:T(8,128)(2,1)S(1)} %all_gather.9.source), custom_call_target="tpu_custom_call" | custom-call | bytes 9963000 | tf_op jit(solution)/shard_map/forward_sums/pallas_call | solution.py:48
  26.2 0.0 copy-start
  26.2 0.0 copy-start.1
  26.2 0.0 copy-start.2
  26.2 0.0 copy-start.3
  26.2 0.0 copy-start.4
  26.2 18.0 %all_to_all.35.arrived = bf16[4,8,128,128]{3,2,1,0:T(8,128)(2,1)S(1)} all-to-all(bf16[4,8,128,128]{3,2,1,0:T(8,128)(2,1)S(1)} %bitcast.36), channel_id=1, replica_groups=mesh['z'=8,'x'=4,'y'=8,'core'=2] {'x'}, dimensions={0} | all-to-all | bytes 2097152 | tf_op jit(solution)/shard_map/all_to_all | solution.py:272
  44.2 0.1 add_pieces.1
  44.3 19.0 %all_to_all.36.pieces = bf16[8,128,128]{2,1,0:T(8,128)(2,1)S(1)} all-to-all(bf16[8,128,128]{2,1,0:T(8,128)(2,1)S(1)} %add_pieces.1), channel_id=1, replica_groups=mesh['z'=8,'x'=4,'y'=8,'core'=2] {'z'}, dimensions={0} | all-to-all | bytes 524288 | tf_op jit(solution)/shard_map/all_to_all | solution.py:272
  63.4 0.0 copy-done
  63.4 0.0 copy-done.1
  63.4 0.0 copy-done.2
  63.4 0.0 copy-done.3
  63.4 0.0 copy-done.4
  63.4 0.4 dense_layer.1
  63.9 9.6 %all_to_all.37.grads = bf16[8,32,128]{2,1,0:T(8,128)(2,1)S(1)} all-to-all(bf16[8,32,128]{2,1,0:T(8,128)(2,1)S(1)} %get-tuple-element.11), channel_id=1, replica_groups=mesh['z'=8,'x'=4,'y'=8,'core'=2] {'y'}, dimensions={0} | all-to-all | bytes 131072 | tf_op jit(solution)/shard_map/all_to_all | solution.py:272
  73.5 12.6 %all_to_all.38.arrived = bf16[8,160,128]{2,1,0:T(8,128)(2,1)S(1)} all-to-all(bf16[8,160,128]{2,1,0:T(8,128)(2,1)S(1)} %pack.1), channel_id=1, replica_groups=mesh['z'=8,'x'=4,'y'=8,'core'=2] {'z'}, dimensions={0} | all-to-all | bytes 655360 | tf_op jit(solution)/shard_map/all_to_all | solution.py:272
  86.1 0.1 relay.1
  86.2 12.3 %all_to_all.39.spread = bf16[4,1056,128]{2,1,0:T(8,128)(2,1)S(1)} all-to-all(bf16[4,1056,128]{2,1,0:T(8,128)(2,1)S(1)} %relay.1), channel_id=1, replica_groups=mesh['z'=8,'x'=4,'y'=8,'core'=2] {'x'}, dimensions={0} | all-to-all | bytes 2162688 | tf_op jit(solution)/shard_map/all_to_all | solution.py:272
  98.6 1.5 %backward_sums.1 = bf16[8,288,128]{2,1,0:T(8,128)(2,1)S(1)} custom-call(s32[5,64]{1,0:T(8,128)S(1)} %stack.2.whole, bf16[64,128,128]{2,1,0:T(8,128)(2,1)S(1)} %convert_bitcast_fusion.bits, bf16[4,1056,128]{2,1,0:T(8,128)(2,1)S(1)} %all_to_all.39.spread), custom_call_target="tpu_custom_call" | custom-call | bytes 5535000 | tf_op jit(solution)/shard_map/backward_sums/pallas_call | solution.py:200
  100.1 15.3 %all_to_all.40.arrived = bf16[8,288,128]{2,1,0:T(8,128)(2,1)S(1)} all-to-all(bf16[8,288,128]{2,1,0:T(8,128)(2,1)S(1)} %backward_sums.1), channel_id=1, replica_groups=mesh['z'=8,'x'=4,'y'=8,'core'=2] {'y'}, dimensions={0} | all-to-all | bytes 1179648 | tf_op jit(solution)/shard_map/all_to_all | solution.py:272
  115.4 0.1 collect.1
  115.5 9.5 %all-gather = bf16[768,128]{1,0:T(8,128)(2,1)S(1)} all-gather(bf16[384,128]{1,0:T(8,128)(2,1)S(1)} %get-tuple-element.13), channel_id=2, replica_groups=mesh['z'=8,'x'=4,'y'=8,'core'=2] {'core'}, dimensions={0}, use_global_device_ids=true | all-gather | bytes 294912 | tf_op jit(solution)/shard_map/all_gather | solution.py:318
  125.0 0.7 final.1
  (3 shorter events, 0.1 us)
Async XLA Ops:
  2.1 17.1 %all-to-all-start = ((bf16[8,128,128]{2,1,0:T(8,128)(2,1)}), bf16[8,128,128]{2,1,0:T(8,128)(2,1)S(1)}, u32[]{:S(2)}, u32[]{:S(2)}) async-start(bf16[8,128,128]{2,1,0:T(8,128)(2,1)} %broadcast_in_dim.12), calls=%async_computation | async-start | bytes 524288 | tf_op jit(solution)/shard_map/all_to_all | solution.py:272
  26.2 37.2 %copy-start = (bf16[128,128]{1,0:T(8,128)(2,1)S(1)}, bf16[128,128]{1,0:T(8,128)(2,1)}, u32[]{:S(2)}) copy-start(bf16[128,128]{1,0:T(8,128)(2,1)} %features.1) | copy-start | bytes 98308
  26.2 37.2 %copy-start.1 = (bf16[128,128]{1,0:T(8,128)(2,1)S(1)}, bf16[128,128]{1,0:T(8,128)(2,1)}, u32[]{:S(2)}) copy-start(bf16[128,128]{1,0:T(8,128)(2,1)} %cotangent.1) | copy-start | bytes 98308
  26.2 37.2 %copy-start.2 = (bf16[128,128]{1,0:T(8,128)(2,1)S(1)}, bf16[128,128]{1,0:T(8,128)(2,1)}, u32[]{:S(2)}) copy-start(bf16[128,128]{1,0:T(8,128)(2,1)} %self_weight.1) | copy-start | bytes 98308
  26.2 37.2 %copy-start.3 = (bf16[128,128]{1,0:T(8,128)(2,1)S(1)}, bf16[128,128]{1,0:T(8,128)(2,1)}, u32[]{:S(2)}) copy-start(bf16[128,128]{1,0:T(8,128)(2,1)} %neigh_weight.1) | copy-start | bytes 98308
  26.2 37.2 %copy-start.4 = (s32[128]{0:T(128)S(1)}, s32[128]{0:T(128)}, u32[]{:S(2)}) copy-start(s32[128]{0:T(128)} %param.13) | copy-start | bytes 1540
